TPU v7x, 32 devices: a whole 2x2x4 slice. The times are simulated.
32 devices in a mesh: replica: 4 (over y, x), fsdp: 4 (over z), tensor: 2 (over core).
Axes of the slice: x: 2, y: 2, z: 4, core: 2. Of those that a mesh axis runs over, the one named last changes fastest.
Arguments:
- momentum: float32 [4, 1024, 3584], P('replica', 'fsdp', 'tensor'), may hold values from -600 to 600
- gradient: bfloat16 [4, 1024, 3584], P('replica', 'fsdp', 'tensor'), may hold values from -300 to 300
- right_in: float32 [3584, 256], P(('tensor', 'fsdp')), may hold values from -6 to 6
Outputs:
- left_factor: float32 [1024, 256], P('fsdp')
- right_factor: float32 [3584, 256], P(('tensor', 'fsdp'))
- new_momentum: float32 [4, 1024, 3584], P('replica', 'fsdp', 'tensor')
All inputs are finite; a program needn't handle non-finite values.
Results may differ from a plain program's by a relative error of at most 0.0003.
Values sent between devices are 32-bit elements; how exact they have to be, the bound alone decides.
A program may use at most 64 MiB of HBM per device.

v0:
```python
import math

import jax
import jax.numpy as jnp
from jax import lax
from jax.sharding import PartitionSpec as P


def shards(momentum, gradient, right_in):
    highest = lax.Precision.HIGHEST
    buffer = momentum[0] + gradient[0].astype(jnp.float32)
    row_count = buffer.shape[0]
    col_count = buffer.shape[1]
    replicas = lax.axis_size("replica")
    fsdp_count = lax.axis_size("fsdp")
    tensor_count = lax.axis_size("tensor")
    col_share = col_count // fsdp_count
    partial_value = jnp.dot(
        buffer, lax.all_gather(right_in, "fsdp", axis=0, tiled=True), precision=highest
    )
    partial_value = partial_value / replicas
    projected = lax.psum(partial_value, ("replica", "tensor"))
    gram_matrix = lax.psum(jnp.dot(projected.T, projected, precision=highest), "fsdp")
    factor_low = jnp.linalg.cholesky(gram_matrix)
    orthonormal = jax.scipy.linalg.solve_triangular(factor_low, projected.T, lower=True).T
    back_terms = jnp.dot(buffer.T, orthonormal, precision=highest) / replicas
    back_proj = lax.psum(back_terms, ("replica", "fsdp"))
    squares = lax.psum(jnp.sum(back_proj * back_proj, axis=0), "tensor")
    own_rows = lax.dynamic_slice_in_dim(back_proj, lax.axis_index("fsdp") * col_share, col_share, 0)
    column_norm = jnp.sqrt(squares + 1e-06)
    right_factor = own_rows * (math.sqrt(col_count * tensor_count) / column_norm)[None, :]
    left_factor = orthonormal * math.sqrt(row_count * fsdp_count)
    new_momentum = buffer - 0.1 * jnp.dot(orthonormal, back_proj.T, precision=highest)
    return (left_factor, right_factor, new_momentum[None])


def solution(mesh):
    placed = (
        P("replica", "fsdp", "tensor"),
        P("replica", "fsdp", "tensor"),
        P(("tensor", "fsdp"), None),
    )
    return jax.shard_map(
        shards,
        mesh=mesh,
        in_specs=placed,
        out_specs=(P("fsdp", None), P(("tensor", "fsdp"), None), P("replica", "fsdp", "tensor")),
        check_vma=False,
    )
```

profile of v0, /device:TPU:17, one launch (start us, length us, event | category | flops | bytes accessed | tf_op | source)
XLA Modules:
  0.0 360.2 jit_solution(2179630357091835158)
XLA Ops:
  7.2 0.7 all-gather.2.cloned.1.call-update
  7.9 43.0 %all-gather.2.cloned.1.call-done = f32[1792,256]{1,0:T(8,128)} async-done(((f32[448,256]{1,0:T(8,128)}), f32[1792,256]{1,0:T(8,128)}) %all-gather.2.cloned.1.call-update) | async-done | bytes 1835024 | tf_op jit(solution)/shard_map/all_gather | solution.py:19
  50.9 4.8 %fusion.5 = f32[256,256]{1,0:T(8,128)} fusion(f32[1792,256]{1,0:T(8,128)} %all-gather.2.cloned.1.call-done, f32[1,256,1792]{2,1,0:T(8,128)} %param.3, bf16[1,256,1792]{2,1,0:T(8,128)(2,1)} %param.4), kind=kOutput, calls=%fused_computation.11 | convolution fusion | flops 1410269184 | bytes 4849664 | tf_op jit(solution)/shard_map/dot_general | solution.py:18
  55.8 52.8 %all-reduce.5.cloned.1.call-done = f32[256,256]{1,0:T(8,128)} async-done(((f32[256,256]{1,0:T(8,128)}), f32[256,256]{1,0:T(8,128)}) %all-reduce.5.cloned.1.call-update) | async-done | bytes 262160 | tf_op jit(solution)/shard_map/psum | solution.py:22
  108.7 2.3 fusion.19
  111.3 33.6 %all-reduce.7.cloned.1.call-done = f32[256,256]{0,1:T(8,128)} async-done(((f32[256,256]{0,1:T(8,128)}), f32[256,256]{0,1:T(8,128)}) %all-reduce.7.cloned.1.call-update) | async-done | bytes 262160 | tf_op jit(solution)/shard_map/psum | solution.py:23
  144.8 1.1 copy.7
  145.9 1.0 fusion.8
  147.0 11.7 %cholesky.50 = f32[128,128]{1,0:T(8,128)S(1)} custom-call(f32[128,128]{1,0:T(8,128)S(1)} %cholesky.118), custom_call_target="Cholesky" | custom-call | tf_op jit(solution)/shard_map/jit(cholesky)/cholesky | solution.py:24
  158.8 0.6 copy-done.3
  159.4 10.4 %custom-call.15 = f32[1,128,128]{1,2,0:T(8,128)} custom-call(f32[1,128,128]{2,1,0:T(8,128)S(1)} %get-tuple-element.27), custom_call_target="InvertDiagBlocksLowerTriangular" | custom-call | tf_op jit(solution)/shard_map/jit(cholesky)/cholesky | solution.py:24
  169.8 0.9 cholesky.113
  170.7 1.0 constant_dynamic-update-slice_fusion
  171.7 0.9 convolution_subtract_fusion.1
  172.6 12.5 %cholesky.105 = f32[128,128]{1,0:T(8,128)S(1)} custom-call(f32[128,128]{1,0:T(8,128)} %convolution_subtract_fusion.1), custom_call_target="Cholesky" | custom-call | tf_op jit(solution)/shard_map/jit(cholesky)/cholesky | solution.py:24
  185.2 0.6 compare_reduce_fusion
  187.2 5.4 %while.1 = (s32[]{:T(128)}, f32[256,256]{1,0:T(8,128)S(1)}, s32[2,2]{1,0:T(2,128)S(1)}, f32[2,128,128]{2,1,0:T(8,128)}, s32[]{:T(128)}) while((s32[]{:T(128)}, f32[256,256]{1,0:T(8,128)S(1)}, s32[2,2]{1,0:T(2,128)S(1)}, f32[2,128,128]{2,1,0:T(8,128)}, s32[]{:T(128)}) %tuple.28), condition=%wide.while_cond, body=%wide.while_body.sunk | while | flops 2 | bytes 132705 | solution.py:25
  187.4 0.6 fusion.29
  188.0 2.0 bitcast_dynamic-update-slice_fusion.2
  190.0 0.6 fusion.29
  190.6 2.0 bitcast_dynamic-update-slice_fusion.2
  192.6 20.5 %custom-call.16 = f32[2,128,128]{1,2,0:T(8,128)S(1)} custom-call(f32[2,128,128]{2,1,0:T(8,128)} %get-tuple-element.10), custom_call_target="InvertDiagBlocksLowerTriangular" | custom-call | tf_op jit(solution)/shard_map/jit(_solve_triangular)/triangular_solve | solution.py:25
  213.1 0.3 fusion.9
  213.5 0.4 convolution_subtract_fusion
  213.9 0.3 fusion.12
  214.2 4.3 %convolution_multiply_fusion.1 = f32[1792,256]{1,0:T(8,128)} fusion(f32[1,256,1792]{2,1,0:T(8,128)S(1)} %copy-done, bf16[1,256,1792]{2,1,0:T(8,128)(2,1)S(1)} %copy-done.1, f32[128,256]{1,0:T(8,128)S(1)} %fusion.12, f32[128,256]{1,0:T(8,128)S(1)} %fusion.9), kind=kOutput, calls=%fused_computation.4 | convolution fusion | flops 1410727936 | bytes 4849664 | tf_op jit(solution)/shard_map/dot_general | solution.py:26
  218.5 0.8 copy.8
  219.4 122.1 %all-reduce.9.cloned.1.call-done = f32[1792,256]{1,0:T(8,128)} async-done(((f32[1792,256]{1,0:T(8,128)}), f32[1792,256]{1,0:T(8,128)}) %all-reduce.9.cloned.1.call-update) | async-done | bytes 1835024 | tf_op jit(solution)/shard_map/psum | solution.py:27
  341.4 1.8 multiply_reduce_fusion
  343.2 2.8 psum.31
  346.0 5.8 %fusion.1 = f32[1,256,1792]{2,1,0:T(8,128)} fusion(f32[1792,256]{1,0:T(8,128)} %all-reduce.9.cloned.1.call-done, f32[1,256,1792]{2,1,0:T(8,128)S(1)} %copy-done, bf16[1,256,1792]{2,1,0:T(8,128)(2,1)S(1)} %copy-done.1, f32[128,256]{1,0:T(8,128)S(1)} %fusion.12, f32[128,256]{1,0:T(8,128)S(1)} %fusion.9), kind=kOutput, calls=%fused_computation.5 | convolution fusion | flops 1411186688 | bytes 6684672 | tf_op jit(solution)/shard_map/dot_general | solution.py:33
  351.8 1.8 dynamic-slice_multiply_fusion
  (25 shorter events, 0.6 us)
Async XLA Ops:
  7.2 43.8 %all-gather.2.cloned.1.call-start = ((), (), s32[]{:S(2)}) async-start(), calls=%async_computation | async-start | bytes 2293760 | tf_op jit(solution)/shard_map/all_gather | solution.py:19
  7.9 100.8 %all-reduce.5.cloned.1.call-start = ((), (), s32[]{:S(2)}) async-start(), calls=%async_computation.1 | async-start | bytes 524288 | tf_op jit(solution)/shard_map/psum | solution.py:22
  55.8 89.1 %all-reduce.7.cloned.1.call-start = ((), (), s32[]{:S(2)}) async-start(), calls=%async_computation.2 | async-start | bytes 524288 | tf_op jit(solution)/shard_map/psum | solution.py:23
  111.0 230.4 %all-reduce.9.cloned.1.call-start = ((), (), s32[]{:S(2)}) async-start(), calls=%async_computation.3 | async-start | bytes 3670016 | tf_op jit(solution)/shard_map/psum | solution.py:27
  145.9 67.2 %copy-start.2 = (f32[256,256]{1,0:T(8,128)S(1)}, f32[256,256]{1,0:T(8,128)}, u32[]{:S(2)}) copy-start(f32[256,256]{1,0:T(8,128)} %all-reduce.5.cloned.1.call-done) | copy-start | bytes 786436
  147.0 67.2 %copy-start = (f32[1,256,1792]{2,1,0:T(8,128)S(1)}, f32[1,256,1792]{2,1,0:T(8,128)}, u32[]{:S(2)}) copy-start(f32[1,256,1792]{2,1,0:T(8,128)} %param.3) | copy-start | bytes 5505028
  147.0 67.2 %copy-start.1 = (bf16[1,256,1792]{2,1,0:T(8,128)(2,1)S(1)}, bf16[1,256,1792]{2,1,0:T(8,128)(2,1)}, u32[]{:S(2)}) copy-start(bf16[1,256,1792]{2,1,0:T(8,128)(2,1)} %param.4) | copy-start | bytes 2752516
  158.7 0.6 copy-start.3
Sparse Core Ops, SparseCore 0:
  9.6 41.3 all-gather.1
  55.9 52.6 all-reduce.4
  111.7 33.1 all-reduce.6
  218.6 122.7 all-reduce.8
where the time goes:
time: 363 us; the launch traced here: 360 us
  waiting for transfers between devices  252 us (69%)
  other arithmetic  60.6 us (17%)
  matrix products  20.2 us (6%)
  between operations  15.2 us (4%)
  local copies, waits for them, and re-layouts  8.67 us (2%)
    psum x1, waiting for transfers between devices, shards(): back_proj = lax.psum(back_terms, ('replica', 'fsdp'))  122 us
    psum x1, waiting for transfers between devices, shards(): projected = lax.psum(partial_value, ('replica', 'tensor'))  52.8 us
    all_gather x1, waiting for transfers between devices, shards(): lax.all_gather(right_in, 'fsdp', axis=0, tiled=True)  43 us
    another operation x6, other arithmetic, shards(): factor_low = jnp.linalg.cholesky(gram_matrix)  35.4 us
    psum x1, waiting for transfers between devices, shards(): lax.psum(jnp.dot(projected.T, projected, precision=highest), 'fsdp')  33.6 us
    another operation x3, other arithmetic, shards(): jax.scipy.linalg.solve_triangular(factor_low, projected.T, lower=True)  20.5 us
  transfers between devices with their start and end apart: 4, of which 4 were waited for; matrix products, arithmetic and copies ran while one was open for 0% of the time, Pallas kernels for 0%

commit v1 on v0

v1 whole, which is shorter than its diff:
```python
import math

import jax
import jax.numpy as jnp
from jax import lax
from jax.experimental import pallas as pl
from jax.experimental.pallas import tpu as pltpu
from jax.sharding import PartitionSpec as P

MESH = pl.DeviceIdType.MESH
HIGHEST = lax.Precision.HIGHEST
F32 = jnp.float32


def dot(a, b, ca, cb):
    return lax.dot_general(
        a, b, (((ca,), (cb,)), ((), ())), precision=HIGHEST, preferred_element_type=F32
    )


def vmem(n):
    return [pl.BlockSpec(memory_space=pltpu.VMEM)] * n


class Place:
    def __init__(self, R, F, T):
        self.R, self.F, self.T, self.n = R, F, T, R * T
        self.r = lax.axis_index("replica")
        self.f = lax.axis_index("fsdp")
        self.t = lax.axis_index("tensor")
        self.p = self.r * T + self.t

    def plane(self, d):
        q = lax.rem(self.p + d, self.n)
        return q, {"replica": q // self.T, "tensor": lax.rem(q, self.T)}

    def plane_from(self, d):
        return lax.rem(self.p + self.n - d, self.n)

    def line(self, d):
        q = lax.rem(self.f + d, self.F)
        return q, {"fsdp": q}

    def line_from(self, d):
        return lax.rem(self.f + self.F - d, self.F)

    def rep(self, d):
        q = lax.rem(self.r + d, self.R)
        return q, {"replica": q}

    def rep_from(self, d):
        return lax.rem(self.r + self.R - d, self.R)


def remote(src, dst, send, recv, where):
    return pltpu.make_async_remote_copy(
        src_ref=src, dst_ref=dst, send_sem=send, recv_sem=recv, device_id=where, device_id_type=MESH
    )


def greet(targets):
    barrier = pltpu.get_barrier_semaphore()
    for where in targets:
        pl.semaphore_signal(barrier, inc=1, device_id=where, device_id_type=MESH)
    pl.semaphore_wait(barrier, len(targets))


def project_kernel(
    R, F, T, mom, grad, q_in, bmean_out, proj_out, gram_out,
    bufs, brecv, qs, pp, precv, proj, gp, grecv, gram,
    b_send, b_recv, q_up, q_down, q_recv, p_send, p_recv, a_send, a_recv,
    g_send, g_recv, h_send, h_recv,
):
    at = Place(R, F, T)
    rows, cols = mom.shape[1], mom.shape[2]
    share = cols // R
    n = at.n
    piece = rows // n
    for k in range(R):
        part = slice(k * share, (k + 1) * share)
        bufs[k] = mom[0, :, part] + grad[0, :, part].astype(F32)
    nb = F // R
    qb = q_in.shape[0]
    nc, qc = qs.shape[1], qs.shape[2]
    for j in range(nb):
        @pl.when(at.f == at.r * nb + j)
        def _():
            for c in range(nc):
                qs[j, c] = q_in[c * qc:(c + 1) * qc, :]

    greet([at.plane(d)[1] for d in range(1, n)] + [at.line(d)[1] for d in range(1, F)])

    sent = []
    for d in range(1, R):
        k, where = at.rep(d)
        copy = remote(bufs.at[k], brecv.at[at.r], b_send.at[d - 1], b_recv.at[at.r], where)
        copy.start()
        sent.append(copy)

    def up(j, c):
        return remote(qs.at[j, c], qs.at[j, c], q_up.at[j, c], q_recv.at[j, c], {"fsdp": lax.rem(at.f + 1, F)})

    def down(j, c):
        return remote(qs.at[j, c], qs.at[j, c], q_down.at[j, c], q_recv.at[j, c], {"fsdp": lax.rem(at.f + F - 1, F)})

    for c in range(nc):
        for j in range(nb):
            home = at.r * nb + j
            @pl.when(at.f != home)
            def _():
                up(j, c).wait_recv()
            @pl.when((at.f >= home) & (at.f < F - 1))
            def _():
                up(j, c).start()
            @pl.when((at.f <= home) & (at.f > 0))
            def _():
                down(j, c).start()

    brecv[at.r] = bufs[at.r]
    for d in range(1, R):
        k = at.rep_from(d)
        remote(bufs.at[k], brecv.at[k], b_send.at[d - 1], b_recv.at[k], at.rep(d)[1]).wait_recv()
    total = brecv[0]
    for k in range(1, R):
        total = total + brecv[k]
    bmean = total * (1.0 / R)
    bmean_out[...] = bmean
    part = dot(bmean, qs[...].reshape(share, q_in.shape[1]), 1, 0)
    pp[...] = part.reshape(pp.shape)

    for d in range(1, n):
        q, where = at.plane(d)
        copy = remote(pp.at[q], precv.at[at.p], p_send.at[d - 1], p_recv.at[at.p], where)
        copy.start()
        sent.append(copy)
    precv[at.p] = pp[at.p]
    for d in range(1, n):
        q = at.plane_from(d)
        remote(pp.at[q], precv.at[q], p_send.at[d - 1], p_recv.at[q], at.plane(d)[1]).wait_recv()
    total = precv[0]
    for k in range(1, n):
        total = total + precv[k]
    proj[at.p] = total
    for d in range(1, n):
        q, where = at.plane(d)
        copy = remote(proj.at[at.p], proj.at[at.p], a_send.at[d - 1], a_recv.at[at.p], where)
        copy.start()
        sent.append(copy)
    for d in range(1, n):
        q = at.plane_from(d)
        remote(proj.at[q], proj.at[q], a_send.at[d - 1], a_recv.at[q], at.plane(d)[1]).wait_recv()
    whole = proj[...].reshape(rows, q_in.shape[1])
    proj_out[...] = whole

    gp[...] = dot(whole, whole, 0, 0).reshape(gp.shape)
    for d in range(1, F):
        q, where = at.line(d)
        copy = remote(gp.at[at.p], grecv.at[at.f], g_send.at[d - 1], g_recv.at[at.f], where)
        copy.start()
        sent.append(copy)
    grecv[at.f] = gp[at.p]
    for d in range(1, F):
        q = at.line_from(d)
        remote(gp.at[at.p], grecv.at[q], g_send.at[d - 1], g_recv.at[q], at.line(d)[1]).wait_recv()
    total = grecv[0]
    for k in range(1, F):
        total = total + grecv[k]
    gram[at.p] = total
    for d in range(1, n):
        q, where = at.plane(d)
        copy = remote(gram.at[at.p], gram.at[at.p], h_send.at[d - 1], h_recv.at[at.p], where)
        copy.start()
        sent.append(copy)
    for d in range(1, n):
        q = at.plane_from(d)
        remote(gram.at[q], gram.at[q], h_send.at[d - 1], h_recv.at[q], at.plane(d)[1]).wait_recv()
    gram_out[...] = gram[...].reshape(gram_out.shape)

    for copy in sent:
        copy.wait_send()
    for c in range(nc):
        for j in range(nb):
            home = at.r * nb + j
            @pl.when((at.f >= home) & (at.f < F - 1))
            def _():
                up(j, c).wait_send()
            @pl.when((at.f <= home) & (at.f > 0))
            def _():
                down(j, c).wait_send()


def eliminate(tile, side):
    b = tile.shape[0]
    rows_id = lax.broadcasted_iota(jnp.int32, tile.shape, 0)
    lanes = lax.broadcasted_iota(jnp.int32, tile.shape, 1)
    other = b - side
    inside = (lanes >= side) & (lanes < side + b)
    x = jnp.where(inside, tile, jnp.where(lanes - other == rows_id, 1.0, 0.0).astype(F32))
    done = []
    for k0 in range(0, b, 8):
        shape = x.shape
        ids = lax.broadcasted_iota(jnp.int32, shape, 0)
        panel = [
            jnp.broadcast_to(x[:, side + k0 + j:side + k0 + j + 1], shape) for j in range(8)
        ]
        for j in range(8):
            inverse = 1.0 / panel[j][j:j + 1, :]
            scale = jnp.where(ids > j, panel[j], 0.0) * inverse
            for i in range(j + 1, 8):
                panel[i] = panel[i] - scale * panel[i][j:j + 1, :]
            x = x - scale * x[j:j + 1, :]
        done.append(x[:8])
        x = x[8:]
    x = jnp.concatenate(done, axis=0)
    pivot = jnp.sum(jnp.where(lanes - side == rows_id, x, 0.0), axis=1, keepdims=True)
    return x * (1.0 / jnp.sqrt(pivot))


def factor_kernel(scale, gram, proj, ortho, left, w):
    size = gram.shape[0]
    b = 64
    w[:, :size] = gram[...]
    ids = lax.broadcasted_iota(jnp.int32, (size, size), 0)
    lanes = lax.broadcasted_iota(jnp.int32, (size, size), 1)
    w[:, size:] = jnp.where(ids == lanes, 1.0, 0.0).astype(F32)
    for o in range(0, size, b):
        base = o // 128 * 128
        side = o - base
        x = eliminate(w[o:o + b, base:base + 128], side)
        block = w[o:o + b, :]
        zero = jnp.zeros_like(block)
        stack = jnp.concatenate([zero, block] if side == 0 else [block, zero], axis=0)
        strip = dot(x, stack, 1, 0)
        w[o:o + b, :] = strip
        if o + b < size:
            update = dot(strip[:, :size], strip, 0, 0)
            w[o + b:, :] = w[o + b:, :] - update[o + b:, :]
    result = dot(proj[...], w[:, size:], 1, 1)
    ortho[...] = result
    left[...] = result * scale


def back_kernel(
    R, F, T, mom, grad, bmean, ortho, right_out, mom_out,
    bp, zrecv, full, sq, sqrecv,
    z_send, z_recv, a_send, a_recv, r_send, r_recv, s_send, s_recv,
):
    at = Place(R, F, T)
    cols = mom.shape[2]
    piece = bp.shape[1]
    rank = ortho.shape[1]
    tens = [{"tensor": lax.rem(at.t + d, T)} for d in range(1, T)]
    back = dot(bmean[...], ortho[...], 0, 0)
    for g in range(F):
        bp[g] = back[g * piece:(g + 1) * piece, :]
    greet([at.rep(d)[1] for d in range(1, R)] + [at.line(d)[1] for d in range(1, F)] + tens)

    sent = []
    for d in range(1, F):
        q, where = at.line(d)
        copy = remote(bp.at[q], zrecv.at[at.f], z_send.at[d - 1], z_recv.at[at.f], where)
        copy.start()
        sent.append(copy)
    zrecv[at.f] = bp[at.f]
    for d in range(1, F):
        q = at.line_from(d)
        remote(bp.at[q], zrecv.at[q], z_send.at[d - 1], z_recv.at[q], at.line(d)[1]).wait_recv()
    total = zrecv[0]
    for k in range(1, F):
        total = total + zrecv[k]
    full[at.r, at.f] = total

    def forward(f, i):
        for d in range(1, R):
            q, where = at.rep(d)
            copy = remote(full.at[at.r, f], full.at[at.r, f], r_send.at[i, d - 1], r_recv.at[at.r, f], where)
            copy.start()
            sent.append(copy)

    forward(at.f, 0)
    for d in range(1, F):
        q, where = at.line(d)
        copy = remote(full.at[at.r, at.f], full.at[at.r, at.f], a_send.at[d - 1], a_recv.at[at.f], where)
        copy.start()
        sent.append(copy)
    for d in range(1, F):
        q = at.line_from(d)
        remote(full.at[at.r, q], full.at[at.r, q], a_send.at[d - 1], a_recv.at[q], at.line(d)[1]).wait_recv()
        forward(q, d)
    for i in range(F):
        g = at.line_from(i)
        for d in range(1, R):
            k = at.rep_from(d)
            remote(full.at[k, g], full.at[k, g], r_send.at[i, d - 1], r_recv.at[k, g], at.rep(d)[1]).wait_recv()

    squares = jnp.zeros((1, rank), F32)
    for k in range(R):
        for g in range(F):
            v = full[k, g]
            squares = squares + jnp.sum(v * v, axis=0, keepdims=True)
    sq[...] = jnp.broadcast_to(squares, sq.shape)
    for d in range(1, T):
        copy = remote(sq, sqrecv.at[at.t], s_send.at[d - 1], s_recv.at[at.t], tens[d - 1])
        copy.start()
        sent.append(copy)
    sqrecv[at.t] = sq[...]

    o = ortho[...] * -0.1
    for k in range(R):
        if (k + 1) % 2:
            continue
        block = jnp.concatenate([full[j, g] for j in (k - 1, k) for g in range(F)], axis=0)
        span = block.shape[0]
        first = (k - 1) // 2 * span
        here = slice(first, first + span)
        mom_out[0, :, here] = mom[0, :, here] + grad[0, :, here].astype(F32) + dot(o, block, 1, 1)

    for d in range(1, T):
        k = lax.rem(at.t + T - d, T)
        remote(sq, sqrecv.at[k], s_send.at[d - 1], s_recv.at[k], tens[d - 1]).wait_recv()
    total = sqrecv[0]
    for k in range(1, T):
        total = total + sqrecv[k]
    norm = jnp.sqrt(total[0:1, :] + 1e-06)
    scale = math.sqrt(cols * T) / norm
    for i in range(R):
        k = at.f * R + i
        right_out[i * piece:(i + 1) * piece, :] = full[k // F, lax.rem(k, F)] * scale
    for copy in sent:
        copy.wait_send()


def solution(mesh):
    R, F, T = mesh.shape["replica"], mesh.shape["fsdp"], mesh.shape["tensor"]
    n = R * T
    DMA = pltpu.SemaphoreType.DMA

    def shards(momentum, gradient, right_in):
        rows, cols = momentum.shape[1], momentum.shape[2]
        qb, rank = right_in.shape
        share = cols // R
        nb = F // R
        nc = 4 if qb % 32 == 0 else 1
        piece = share // F
        sds = jax.ShapeDtypeStruct
        slots = lambda m, r: pltpu.VMEM((m, r, rank), F32)
        bmean, proj, gram = pl.pallas_call(
            lambda *refs: project_kernel(R, F, T, *refs),
            out_shape=(sds((rows, share), F32), sds((rows, rank), F32), sds((rank, rank), F32)),
            in_specs=vmem(3),
            out_specs=tuple(vmem(3)),
            scratch_shapes=[
                pltpu.VMEM((R, rows, share), F32),
                pltpu.VMEM((R, rows, share), F32),
                pltpu.VMEM((nb, nc, qb // nc, rank), F32),
                slots(n, rows // n),
                slots(n, rows // n),
                slots(n, rows // n),
                slots(n, rank // n),
                slots(F, rank // n),
                slots(n, rank // n),
                DMA((R,)), DMA((R,)),
                DMA((nb, nc)), DMA((nb, nc)), DMA((nb, nc)),
                DMA((n,)), DMA((n,)), DMA((n,)), DMA((n,)),
                DMA((F,)), DMA((F,)), DMA((n,)), DMA((n,)),
            ],
            compiler_params=pltpu.CompilerParams(
                collective_id=0, has_side_effects=True, vmem_limit_bytes=40 << 20
            ),
            name="project",
        )(momentum, gradient, right_in)
        ortho, left = pl.pallas_call(
            lambda *refs: factor_kernel(math.sqrt(rows * F), *refs),
            out_shape=(sds((rows, rank), F32), sds((rows, rank), F32)),
            in_specs=vmem(2),
            out_specs=tuple(vmem(2)),
            scratch_shapes=[pltpu.VMEM((rank, 2 * rank), F32)],
            compiler_params=pltpu.CompilerParams(vmem_limit_bytes=40 << 20),
            name="factor",
        )(gram, proj)
        right, updated = pl.pallas_call(
            lambda *refs: back_kernel(R, F, T, *refs),
            out_shape=(sds((qb, rank), F32), sds(momentum.shape, F32)),
            in_specs=vmem(4),
            out_specs=tuple(vmem(2)),
            scratch_shapes=[
                slots(F, piece),
                slots(F, piece),
                pltpu.VMEM((R, F, piece, rank), F32),
                pltpu.VMEM((8, rank), F32),
                slots(T, 8),
                DMA((F,)), DMA((F,)), DMA((F,)), DMA((F,)),
                DMA((F, R)), DMA((R, F)), DMA((T,)), DMA((T,)),
            ],
            compiler_params=pltpu.CompilerParams(
                collective_id=1, has_side_effects=True, vmem_limit_bytes=40 << 20
            ),
            name="back",
        )(momentum, gradient, bmean, ortho)
        return left, right, updated

    placed = (
        P("replica", "fsdp", "tensor"),
        P("replica", "fsdp", "tensor"),
        P(("tensor", "fsdp"), None),
    )
    return jax.shard_map(
        shards,
        mesh=mesh,
        in_specs=placed,
        out_specs=(P("fsdp", None), P(("tensor", "fsdp"), None), P("replica", "fsdp", "tensor")),
        check_vma=False,
    )
```

time: 363 us -> 107 us (0.29)
  waiting for transfers between devices: 252 us -> 0 us
  Pallas kernels: 0 us -> 99.5 us
  other arithmetic: 60.6 us -> 0 us
  matrix products: 20.2 us -> 0 us
  between operations: 15.2 us -> 0.66 us
    psum x3 -> x0, waiting for transfers between devices: 208 us -> none  [the longest x1 122 us: shards(): back_proj = lax.psum(back_terms, ('replica', 'fsdp'))]
    pallas_call x0 -> x3, Pallas kernels: none -> 99.5 us  [the longest x1 47.8 us: shards(): pl.pallas_call(lambda *refs: project_kernel(R, F, T, *refs), out_shape=(s...]
    another operation x9 -> x0, other arithmetic: 55.9 us -> none  [the longest x6 35.4 us: shards(): factor_low = jnp.linalg.cholesky(gram_matrix)]
    all_gather x1 -> x0, waiting for transfers between devices: 43 us -> none  [shards(): lax.all_gather(right_in, 'fsdp', axis=0, tiled=True)]
    dot_general x4 -> x0, matrix products: 17.2 us -> none  [the longest x1 5.81 us: shards(): jnp.dot(orthonormal, back_proj.T, precision=highest)]
    another operation x9 -> x0, local copies, waits for them, and re-layouts: 6.15 us -> none
    unnamed x9 -> x10, local copies, waits for them, and re-layouts: 1.44 us -> 5.69 us
  transfers between devices with their start and end apart: 4 -> 0, of which waited for: 4 -> 0; matrix products, arithmetic and copies ran while one was open for 0% -> 0% of each run, Pallas kernels for 0% -> 0%
where the time goes in v1:
time: 107 us; the launch traced here: 106 us
  Pallas kernels  99.5 us (93%)
  local copies, waits for them, and re-layouts  5.69 us (5%)
    pallas_call x1, Pallas kernels, shards(): pl.pallas_call(lambda *refs: project_kernel(R, F, T, *refs), out_shape=(s...  47.8 us
    pallas_call x1, Pallas kernels, shards(): pl.pallas_call(lambda *refs: back_kernel(R, F, T, *refs), out_shape=(sds(...  40.7 us
    pallas_call x1, Pallas kernels, shards(): pl.pallas_call(lambda *refs: factor_kernel(math.sqrt(rows * F), *refs), o...  11 us
    unnamed x10, local copies, waits for them, and re-layouts  5.69 us

profile of v1, /device:TPU:17, one launch (start us, length us, event | category | flops | bytes accessed | tf_op | source)
XLA Modules:
  0.0 105.8 jit_solution(2557009068267698624)
XLA Ops:
  0.6 0.0 copy-start
  0.6 1.5 %copy-done = f32[1,256,1792]{2,1,0:T(8,128)S(1)} copy-done((f32[1,256,1792]{2,1,0:T(8,128)S(1)}, f32[1,256,1792]{2,1,0:T(8,128)}, u32[]{:S(2)}) %copy-start) | copy-done | bytes 1835032
  2.1 0.0 copy-start.2
  2.1 1.2 %copy-done.2 = bf16[1,256,1792]{2,1,0:T(8,128)(2,1)S(1)} copy-done((bf16[1,256,1792]{2,1,0:T(8,128)(2,1)S(1)}, bf16[1,256,1792]{2,1,0:T(8,128)(2,1)}, u32[]{:S(2)}) %copy-start.2) | copy-done | bytes 917528
  3.3 0.0 copy-start.3
  3.3 1.0 copy-done.3
  4.3 0.0 copy-start.1
  4.3 47.8 %project.1 = (f32[256,448]{1,0:T(8,128)S(1)}, f32[256,256]{1,0:T(8,128)S(1)}, f32[256,256]{1,0:T(8,128)S(1)}) custom-call(f32[1,256,1792]{2,1,0:T(8,128)S(1)} %copy-done, bf16[1,256,1792]{2,1,0:T(8,128)(2,1)S(1)} %copy-done.2, f32[448,256]{1,0:T(8,128)S(1)} %copy-done.3), custom_call_target="tpu_custom_call" | custom-call | tf_op jit(solution)/shard_map/project/pallas_call | solution.py:347
  52.1 11.0 %factor.1 = (f32[256,256]{1,0:T(8,128)S(1)}, f32[256,256]{1,0:T(8,128)}) custom-call(f32[256,256]{1,0:T(8,128)S(1)} %get-tuple-element.10.refs_0_, f32[256,256]{1,0:T(8,128)S(1)} %get-tuple-element.11.refs_1_), custom_call_target="tpu_custom_call" | custom-call | tf_op jit(solution)/shard_map/factor/pallas_call | solution.py:372
  63.1 0.0 copy-done.1
  63.1 40.7 %back.1 = (f32[448,256]{1,0:T(8,128)S(1)}, f32[1,256,1792]{2,1,0:T(8,128)S(1)}) custom-call(f32[1,256,1792]{2,1,0:T(8,128)S(1)} %copy-done.1, bf16[1,256,1792]{2,1,0:T(8,128)(2,1)S(1)} %copy-done.2, f32[256,448]{1,0:T(8,128)S(1)} %get-tuple-element.13.refs_2_, f32[256,256]{1,0:T(8,128)S(1)} %get-tuple-element.14.refs_3_), custom_call_target="tpu_custom_call" | custom-call | tf_op jit(solution)/shard_map/back/pallas_call | solution.py:381
  103.8 0.8 copy.8
  104.6 1.2 %copy.9 = f32[1,256,1792]{2,1,0:T(8,128)} copy(f32[1,256,1792]{2,1,0:T(8,128)S(1)} %get-tuple-element.22) | data formatting | bytes 3670016
Async XLA Ops:
  0.6 1.5 %copy-start = (f32[1,256,1792]{2,1,0:T(8,128)S(1)}, f32[1,256,1792]{2,1,0:T(8,128)}, u32[]{:S(2)}) copy-start(f32[1,256,1792]{2,1,0:T(8,128)} %refs_0_.3) | copy-start | bytes 5505028
  2.1 1.2 %copy-start.2 = (bf16[1,256,1792]{2,1,0:T(8,128)(2,1)S(1)}, bf16[1,256,1792]{2,1,0:T(8,128)(2,1)}, u32[]{:S(2)}) copy-start(bf16[1,256,1792]{2,1,0:T(8,128)(2,1)} %refs_1_.3) | copy-start | bytes 2752516
  3.3 1.0 copy-start.3
  4.3 58.8 %copy-start.1 = (f32[1,256,1792]{2,1,0:T(8,128)S(1)}, f32[1,256,1792]{2,1,0:T(8,128)}, u32[]{:S(2)}) copy-start(f32[1,256,1792]{2,1,0:T(8,128)} %refs_0_.3) | copy-start | bytes 5505028

commit v2 on v1

--- a/solution.py
+++ b/solution.py
@@ -20,6 +20,10 @@
 
 def vmem(n):
     return [pl.BlockSpec(memory_space=pltpu.VMEM)] * n
+
+
+def hbm(n):
+    return [pl.BlockSpec(memory_space=pl.ANY)] * n
 
 
 class Place:
@@ -44,6 +48,10 @@
     def line_from(self, d):
         return lax.rem(self.f + self.F - d, self.F)
 
+    def cross(self):
+        low = lax.rem(self.r, 2)
+        return self.r + 1 - 2 * low, lax.rem(self.r + 2, 4), 3 - self.r
+
     def rep(self, d):
         q = lax.rem(self.r + d, self.R)
         return q, {"replica": q}
@@ -65,37 +73,75 @@
     pl.semaphore_wait(barrier, len(targets))
 
 
+def pack(part):
+    rows, share = part.shape
+    whole = share // 128 * 128
+    tiles = [part[:, i:i + 128] for i in range(0, whole, 128)]
+    if whole < share:
+        half = rows // 2
+        tiles.append(jnp.concatenate([part[:half, whole:], part[half:, whole:]], axis=1))
+    return jnp.concatenate(tiles, axis=0)
+
+
+def unpack(flat, rows, share):
+    whole = share // 128 * 128
+    tiles = [flat[i * rows:(i + 1) * rows] for i in range(whole // 128)]
+    if whole < share:
+        last = flat[whole // 128 * rows:]
+        tiles.append(jnp.concatenate([last[:, :64], last[:, 64:]], axis=0))
+    return jnp.concatenate(tiles, axis=1)
+
+
 def project_kernel(
-    R, F, T, mom, grad, q_in, bmean_out, proj_out, gram_out,
-    bufs, brecv, qs, pp, precv, proj, gp, grecv, gram,
-    b_send, b_recv, q_up, q_down, q_recv, p_send, p_recv, a_send, a_recv,
+    R, F, T, mom_in, grad_in, q_in, bmean_out, proj_out, gram_out,
+    mom, grad, bufs, brecv, qs, pp, precv, proj, gp, grecv, gram,
+    in_sem, q_sem, b_send, b_recv, q_up, q_down, q_recv, p_send, p_recv, a_send, a_recv,
     g_send, g_recv, h_send, h_recv,
 ):
     at = Place(R, F, T)
-    rows, cols = mom.shape[1], mom.shape[2]
+    rows, cols = mom.shape
     share = cols // R
     n = at.n
-    piece = rows // n
-    for k in range(R):
-        part = slice(k * share, (k + 1) * share)
-        bufs[k] = mom[0, :, part] + grad[0, :, part].astype(F32)
+    loads = [
+        pltpu.make_async_copy(mom_in.at[0], mom, in_sem.at[0]),
+        pltpu.make_async_copy(grad_in.at[0], grad, in_sem.at[1]),
+    ]
+    for copy in loads:
+        copy.start()
     nb = F // R
-    qb = q_in.shape[0]
     nc, qc = qs.shape[1], qs.shape[2]
+
+    def fetch(j, c):
+        return pltpu.make_async_copy(q_in.at[pl.ds(c * qc, qc)], qs.at[j, c], q_sem.at[j, c])
+
     for j in range(nb):
         @pl.when(at.f == at.r * nb + j)
         def _():
             for c in range(nc):
-                qs[j, c] = q_in[c * qc:(c + 1) * qc, :]
+                fetch(j, c).start()
 
     greet([at.plane(d)[1] for d in range(1, n)] + [at.line(d)[1] for d in range(1, F)])
 
+    for copy in loads:
+        copy.wait()
+    half = bufs.shape[2]
+    for k in range(R):
+        part = slice(k * share, (k + 1) * share)
+        flat = pack(mom[:, part] + grad[:, part].astype(F32))
+        for h in range(2):
+            bufs[k, h] = flat[h * half:(h + 1) * half]
+
+    rx, ry, rd = at.cross()
     sent = []
-    for d in range(1, R):
-        k, where = at.rep(d)
-        copy = remote(bufs.at[k], brecv.at[at.r], b_send.at[d - 1], b_recv.at[at.r], where)
-        copy.start()
-        sent.append(copy)
+
+    def hop(src, h, slot, k):
+        return remote(bufs.at[src, h], brecv.at[h, slot], b_send.at[h, slot], b_recv.at[h, slot], {"replica": k})
+
+    for slot in range(2):
+        for h, first in enumerate((rx, ry)):
+            copy = hop((rd, first)[slot], h, slot, first)
+            copy.start()
+            sent.append(copy)
 
     def up(j, c):
         return remote(qs.at[j, c], qs.at[j, c], q_up.at[j, c], q_recv.at[j, c], {"fsdp": lax.rem(at.f + 1, F)})
@@ -103,27 +149,37 @@
     def down(j, c):
         return remote(qs.at[j, c], qs.at[j, c], q_down.at[j, c], q_recv.at[j, c], {"fsdp": lax.rem(at.f + F - 1, F)})
 
+    def pass_on(c, j):
+        home = at.r * nb + j
+        @pl.when(at.f == home)
+        def _():
+            fetch(j, c).wait()
+        @pl.when(at.f != home)
+        def _():
+            up(j, c).wait_recv()
+        @pl.when((at.f >= home) & (at.f < F - 1))
+        def _():
+            up(j, c).start()
+        @pl.when((at.f <= home) & (at.f > 0))
+        def _():
+            down(j, c).start()
+
     for c in range(nc):
         for j in range(nb):
-            home = at.r * nb + j
-            @pl.when(at.f != home)
-            def _():
-                up(j, c).wait_recv()
-            @pl.when((at.f >= home) & (at.f < F - 1))
-            def _():
-                up(j, c).start()
-            @pl.when((at.f <= home) & (at.f > 0))
-            def _():
-                down(j, c).start()
-
-    brecv[at.r] = bufs[at.r]
-    for d in range(1, R):
-        k = at.rep_from(d)
-        remote(bufs.at[k], brecv.at[k], b_send.at[d - 1], b_recv.at[k], at.rep(d)[1]).wait_recv()
-    total = brecv[0]
-    for k in range(1, R):
-        total = total + brecv[k]
-    bmean = total * (1.0 / R)
+            pass_on(c, j)
+        if c == 0:
+            for h, second in enumerate((ry, rx)):
+                hop(rd, h, 0, second).wait_recv()
+                bufs[second, h] = bufs[second, h] + brecv[h, 0]
+                copy = hop(second, h, 2, second)
+                copy.start()
+                sent.append(copy)
+    for h, (first, second) in enumerate(((rx, ry), (ry, rx))):
+        hop(first, h, 1, first).wait_recv()
+    for h, second in enumerate((ry, rx)):
+        hop(second, h, 2, second).wait_recv()
+    flat = jnp.concatenate([bufs[at.r, h] + brecv[h, 1] + brecv[h, 2] for h in range(2)], axis=0)
+    bmean = unpack(flat * (1.0 / R), rows, share)
     bmean_out[...] = bmean
     part = dot(bmean, qs[...].reshape(share, q_in.shape[1]), 1, 0)
     pp[...] = part.reshape(pp.shape)
@@ -241,83 +297,117 @@
 
 
 def back_kernel(
-    R, F, T, mom, grad, bmean, ortho, right_out, mom_out,
-    bp, zrecv, full, sq, sqrecv,
-    z_send, z_recv, a_send, a_recv, r_send, r_recv, s_send, s_recv,
+    R, F, T, mom_in, grad_in, bmean, ortho, right_out, mom_out,
+    mom, grad, bp, zrecv, full, sq, sqrecv,
+    in_sem, out_sem, z_send, z_recv, a_send, a_recv, r_send, r_recv, x_send, s_send, s_recv,
 ):
     at = Place(R, F, T)
-    cols = mom.shape[2]
-    piece = bp.shape[1]
+    loads = [
+        pltpu.make_async_copy(mom_in.at[0], mom, in_sem.at[0]),
+        pltpu.make_async_copy(grad_in.at[0], grad, in_sem.at[1]),
+    ]
+    for copy in loads:
+        copy.start()
+    cols = mom.shape[1]
+    parts, sub = bp.shape[1], bp.shape[2]
+    piece = parts * sub
     rank = ortho.shape[1]
     tens = [{"tensor": lax.rem(at.t + d, T)} for d in range(1, T)]
+    rx, ry, rd = at.cross()
     back = dot(bmean[...], ortho[...], 0, 0)
     for g in range(F):
-        bp[g] = back[g * piece:(g + 1) * piece, :]
-    greet([at.rep(d)[1] for d in range(1, R)] + [at.line(d)[1] for d in range(1, F)] + tens)
+        for h in range(parts):
+            bp[g, h] = back[g * piece + h * sub:g * piece + (h + 1) * sub, :]
+    greet([{"replica": rx}, {"replica": ry}] + [at.line(d)[1] for d in range(1, F)] + tens)
 
     sent = []
-    for d in range(1, F):
-        q, where = at.line(d)
-        copy = remote(bp.at[q], zrecv.at[at.f], z_send.at[d - 1], z_recv.at[at.f], where)
+
+    def go(copy):
         copy.start()
         sent.append(copy)
-    zrecv[at.f] = bp[at.f]
-    for d in range(1, F):
-        q = at.line_from(d)
-        remote(bp.at[q], zrecv.at[q], z_send.at[d - 1], z_recv.at[q], at.line(d)[1]).wait_recv()
-    total = zrecv[0]
-    for k in range(1, F):
-        total = total + zrecv[k]
-    full[at.r, at.f] = total
-
-    def forward(f, i):
-        for d in range(1, R):
-            q, where = at.rep(d)
-            copy = remote(full.at[at.r, f], full.at[at.r, f], r_send.at[i, d - 1], r_recv.at[at.r, f], where)
-            copy.start()
-            sent.append(copy)
-
-    forward(at.f, 0)
-    for d in range(1, F):
-        q, where = at.line(d)
-        copy = remote(full.at[at.r, at.f], full.at[at.r, at.f], a_send.at[d - 1], a_recv.at[at.f], where)
-        copy.start()
-        sent.append(copy)
-    for d in range(1, F):
-        q = at.line_from(d)
-        remote(full.at[at.r, q], full.at[at.r, q], a_send.at[d - 1], a_recv.at[q], at.line(d)[1]).wait_recv()
-        forward(q, d)
-    for i in range(F):
+
+    for h in range(parts):
+        for d in range(1, F):
+            q, where = at.line(d)
+            go(remote(bp.at[q, h], zrecv.at[at.f, h], z_send.at[h, d], z_recv.at[h, at.f], where))
+
+    def share_out(h, i):
         g = at.line_from(i)
-        for d in range(1, R):
-            k = at.rep_from(d)
-            remote(full.at[k, g], full.at[k, g], r_send.at[i, d - 1], r_recv.at[k, g], at.rep(d)[1]).wait_recv()
+        slot = full.at[at.r, g, h]
+        for e, k in enumerate((rx, ry)):
+            go(remote(slot, slot, r_send.at[h, i, e], r_recv.at[at.r, g, h], {"replica": k}))
+
+    def arrive(k, g, h):
+        slot = full.at[k, g, h]
+        remote(slot, slot, r_send.at[h, 0, 0], r_recv.at[k, g, h], {"replica": rx}).wait_recv()
+
+    def cross_on(h, i):
+        g = at.line_from(i)
+        odd = lax.rem(g, 2)
+        arrive(rx, g, h)
+        arrive(ry, g, h)
+        src = rx + (ry - rx) * odd
+        dst = ry + (rx - ry) * odd
+        slot = full.at[src, g, h]
+        go(remote(slot, slot, x_send.at[h, i], r_recv.at[src, g, h], {"replica": dst}))
+
+    for h in range(parts):
+        zrecv[at.f, h] = bp[at.f, h]
+        for d in range(1, F):
+            q = at.line_from(d)
+            remote(bp.at[q, h], zrecv.at[q, h], z_send.at[h, d], z_recv.at[h, q], at.line(d)[1]).wait_recv()
+        total = zrecv[0, h]
+        for k in range(1, F):
+            total = total + zrecv[k, h]
+        full[at.r, at.f, h] = total
+        slot = full.at[at.r, at.f, h]
+        for d in range(1, F):
+            q, where = at.line(d)
+            go(remote(slot, slot, a_send.at[h, d], a_recv.at[h, at.f], where))
+        share_out(h, 0)
+    order = [(h, i) for h in range(parts) for i in range(1, F)]
+    late = [(h, 0) for h in range(parts)]
+    for h, i in order:
+        q = at.line_from(i)
+        slot = full.at[at.r, q, h]
+        remote(slot, slot, a_send.at[h, i], a_recv.at[h, q], at.line(i)[1]).wait_recv()
+        share_out(h, i)
+        late.append((h, i))
+        cross_on(*late.pop(0))
+    for h, i in late:
+        cross_on(h, i)
+    for h in range(parts):
+        for i in range(F):
+            arrive(rd, at.line_from(i), h)
 
     squares = jnp.zeros((1, rank), F32)
     for k in range(R):
         for g in range(F):
-            v = full[k, g]
-            squares = squares + jnp.sum(v * v, axis=0, keepdims=True)
+            for h in range(parts):
+                v = full[k, g, h]
+                squares = squares + jnp.sum(v * v, axis=0, keepdims=True)
     sq[...] = jnp.broadcast_to(squares, sq.shape)
     for d in range(1, T):
-        copy = remote(sq, sqrecv.at[at.t], s_send.at[d - 1], s_recv.at[at.t], tens[d - 1])
-        copy.start()
-        sent.append(copy)
+        go(remote(sq, sqrecv.at[at.t], s_send.at[d], s_recv.at[at.t], tens[d - 1]))
     sqrecv[at.t] = sq[...]
 
+    for copy in loads:
+        copy.wait()
     o = ortho[...] * -0.1
-    for k in range(R):
-        if (k + 1) % 2:
-            continue
-        block = jnp.concatenate([full[j, g] for j in (k - 1, k) for g in range(F)], axis=0)
-        span = block.shape[0]
-        first = (k - 1) // 2 * span
-        here = slice(first, first + span)
-        mom_out[0, :, here] = mom[0, :, here] + grad[0, :, here].astype(F32) + dot(o, block, 1, 1)
+    stores = []
+    for m in range(2):
+        block = jnp.concatenate(
+            [full[k, g, h] for k in range(m * R // 2, (m + 1) * R // 2) for g in range(F) for h in range(parts)], axis=0
+        )
+        here = pl.ds(m * (cols // 2), cols // 2)
+        mom[:, here] = mom[:, here] + grad[:, here].astype(F32) + dot(o, block, 1, 1)
+        copy = pltpu.make_async_copy(mom.at[:, here], mom_out.at[0, :, here], out_sem.at[m])
+        copy.start()
+        stores.append(copy)
 
     for d in range(1, T):
         k = lax.rem(at.t + T - d, T)
-        remote(sq, sqrecv.at[k], s_send.at[d - 1], s_recv.at[k], tens[d - 1]).wait_recv()
+        remote(sq, sqrecv.at[k], s_send.at[d], s_recv.at[k], tens[d - 1]).wait_recv()
     total = sqrecv[0]
     for k in range(1, T):
         total = total + sqrecv[k]
@@ -325,7 +415,11 @@
     scale = math.sqrt(cols * T) / norm
     for i in range(R):
         k = at.f * R + i
-        right_out[i * piece:(i + 1) * piece, :] = full[k // F, lax.rem(k, F)] * scale
+        for h in range(parts):
+            first = i * piece + h * sub
+            right_out[first:first + sub, :] = full[k // F, lax.rem(k, F), h] * scale
+    for copy in stores:
+        copy.wait()
     for copy in sent:
         copy.wait_send()
 
@@ -342,16 +436,19 @@
         nb = F // R
         nc = 4 if qb % 32 == 0 else 1
         piece = share // F
+        parts = 2
         sds = jax.ShapeDtypeStruct
         slots = lambda m, r: pltpu.VMEM((m, r, rank), F32)
         bmean, proj, gram = pl.pallas_call(
             lambda *refs: project_kernel(R, F, T, *refs),
             out_shape=(sds((rows, share), F32), sds((rows, rank), F32), sds((rank, rank), F32)),
-            in_specs=vmem(3),
+            in_specs=hbm(3),
             out_specs=tuple(vmem(3)),
             scratch_shapes=[
-                pltpu.VMEM((R, rows, share), F32),
-                pltpu.VMEM((R, rows, share), F32),
+                pltpu.VMEM((rows, cols), F32),
+                pltpu.VMEM((rows, cols), gradient.dtype),
+                pltpu.VMEM((R, 2, rows * share // 256, 128), F32),
+                pltpu.VMEM((2, 3, rows * share // 256, 128), F32),
                 pltpu.VMEM((nb, nc, qb // nc, rank), F32),
                 slots(n, rows // n),
                 slots(n, rows // n),
@@ -359,7 +456,7 @@
                 slots(n, rank // n),
                 slots(F, rank // n),
                 slots(n, rank // n),
-                DMA((R,)), DMA((R,)),
+                DMA((2,)), DMA((nb, nc)), DMA((2, 3)), DMA((2, 3)),
                 DMA((nb, nc)), DMA((nb, nc)), DMA((nb, nc)),
                 DMA((n,)), DMA((n,)), DMA((n,)), DMA((n,)),
                 DMA((F,)), DMA((F,)), DMA((n,)), DMA((n,)),
@@ -381,16 +478,19 @@
         right, updated = pl.pallas_call(
             lambda *refs: back_kernel(R, F, T, *refs),
             out_shape=(sds((qb, rank), F32), sds(momentum.shape, F32)),
-            in_specs=vmem(4),
-            out_specs=tuple(vmem(2)),
+            in_specs=hbm(2) + vmem(2),
+            out_specs=(vmem(1) + hbm(1)),
             scratch_shapes=[
-                slots(F, piece),
-                slots(F, piece),
-                pltpu.VMEM((R, F, piece, rank), F32),
+                pltpu.VMEM((rows, cols), F32),
+                pltpu.VMEM((rows, cols), gradient.dtype),
+                pltpu.VMEM((F, parts, piece // parts, rank), F32),
+                pltpu.VMEM((F, parts, piece // parts, rank), F32),
+                pltpu.VMEM((R, F, parts, piece // parts, rank), F32),
                 pltpu.VMEM((8, rank), F32),
                 slots(T, 8),
-                DMA((F,)), DMA((F,)), DMA((F,)), DMA((F,)),
-                DMA((F, R)), DMA((R, F)), DMA((T,)), DMA((T,)),
+                DMA((2,)), DMA((2,)),
+                DMA((parts, F)), DMA((parts, F)), DMA((parts, F)), DMA((parts, F)),
+                DMA((parts, F, 2)), DMA((R, F, parts)), DMA((parts, F)), DMA((T,)), DMA((T,)),
             ],
             compiler_params=pltpu.CompilerParams(
                 collective_id=1, has_side_effects=True, vmem_limit_bytes=40 << 20

time: 107 us -> 107 us (level); the launches traced: 106 us -> 105 us
  Pallas kernels: 99.5 us -> 98.3 us
    pallas_call x1, Pallas kernels: 40.7 us -> 39.1 us  [shards(): pl.pallas_call(lambda *refs: back_kernel(R, F, T, *refs), out_shape=(sds(...]
where the time goes in v2:
time: 107 us; the launch traced here: 105 us
  Pallas kernels  98.3 us (92%)
  local copies, waits for them, and re-layouts  5.69 us (5%)
    pallas_call x1, Pallas kernels, shards(): pl.pallas_call(lambda *refs: project_kernel(R, F, T, *refs), out_shape=(s...  48.3 us
    pallas_call x1, Pallas kernels, shards(): pl.pallas_call(lambda *refs: back_kernel(R, F, T, *refs), out_shape=(sds(...  39.1 us
    pallas_call x1, Pallas kernels, shards(): pl.pallas_call(lambda *refs: factor_kernel(math.sqrt(rows * F), *refs), o...  11 us
    unnamed x10, local copies, waits for them, and re-layouts  5.69 us

profile of v2, /device:TPU:17, one launch (start us, length us, event | category | flops | bytes accessed | tf_op | source)
XLA Modules:
  0.0 104.7 jit_solution(10239076794024509104)
XLA Ops:
  0.6 0.0 copy-start
  0.6 1.5 %copy-done = f32[1,256,1792]{2,1,0:T(8,128)S(1)} copy-done((f32[1,256,1792]{2,1,0:T(8,128)S(1)}, f32[1,256,1792]{2,1,0:T(8,128)}, u32[]{:S(2)}) %copy-start) | copy-done | bytes 1835032
  2.1 0.0 copy-start.2
  2.1 1.2 %copy-done.2 = bf16[1,256,1792]{2,1,0:T(8,128)(2,1)S(1)} copy-done((bf16[1,256,1792]{2,1,0:T(8,128)(2,1)S(1)}, bf16[1,256,1792]{2,1,0:T(8,128)(2,1)}, u32[]{:S(2)}) %copy-start.2) | copy-done | bytes 917528
  3.3 0.0 copy-start.3
  3.3 1.0 copy-done.3
  4.3 0.0 copy-start.1
  4.3 48.3 %project.1 = (f32[256,448]{1,0:T(8,128)S(1)}, f32[256,256]{1,0:T(8,128)S(1)}, f32[256,256]{1,0:T(8,128)S(1)}) custom-call(f32[1,256,1792]{2,1,0:T(8,128)S(1)} %copy-done, bf16[1,256,1792]{2,1,0:T(8,128)(2,1)S(1)} %copy-done.2, f32[448,256]{1,0:T(8,128)S(1)} %copy-done.3), custom_call_target="tpu_custom_call" | custom-call | tf_op jit(solution)/shard_map/project/pallas_call | solution.py:442
  52.6 11.0 %factor.1 = (f32[256,256]{1,0:T(8,128)S(1)}, f32[256,256]{1,0:T(8,128)}) custom-call(f32[256,256]{1,0:T(8,128)S(1)} %get-tuple-element.10.refs_0_, f32[256,256]{1,0:T(8,128)S(1)} %get-tuple-element.11.refs_1_), custom_call_target="tpu_custom_call" | custom-call | tf_op jit(solution)/shard_map/factor/pallas_call | solution.py:469
  63.6 0.0 copy-done.1
  63.6 39.1 %back.1 = (f32[448,256]{1,0:T(8,128)S(1)}, f32[1,256,1792]{2,1,0:T(8,128)S(1)}) custom-call(f32[1,256,1792]{2,1,0:T(8,128)S(1)} %copy-done.1, bf16[1,256,1792]{2,1,0:T(8,128)(2,1)S(1)} %copy-done.2, f32[256,448]{1,0:T(8,128)S(1)} %get-tuple-element.13.refs_2_, f32[256,256]{1,0:T(8,128)S(1)} %get-tuple-element.14.refs_3_), custom_call_target="tpu_custom_call" | custom-call | tf_op jit(solution)/shard_map/back/pallas_call | solution.py:478
  102.7 0.8 copy.8
  103.5 1.2 %copy.9 = f32[1,256,1792]{2,1,0:T(8,128)} copy(f32[1,256,1792]{2,1,0:T(8,128)S(1)} %get-tuple-element.22) | data formatting | bytes 3670016
Async XLA Ops:
  0.6 1.5 %copy-start = (f32[1,256,1792]{2,1,0:T(8,128)S(1)}, f32[1,256,1792]{2,1,0:T(8,128)}, u32[]{:S(2)}) copy-start(f32[1,256,1792]{2,1,0:T(8,128)} %refs_0_.3) | copy-start | bytes 5505028
  2.1 1.2 %copy-start.2 = (bf16[1,256,1792]{2,1,0:T(8,128)(2,1)S(1)}, bf16[1,256,1792]{2,1,0:T(8,128)(2,1)}, u32[]{:S(2)}) copy-start(bf16[1,256,1792]{2,1,0:T(8,128)(2,1)} %refs_1_.3) | copy-start | bytes 2752516
  3.3 1.0 copy-start.3
  4.3 59.3 %copy-start.1 = (f32[1,256,1792]{2,1,0:T(8,128)S(1)}, f32[1,256,1792]{2,1,0:T(8,128)}, u32[]{:S(2)}) copy-start(f32[1,256,1792]{2,1,0:T(8,128)} %refs_0_.3) | copy-start | bytes 5505028

commit v3 on v2

--- a/solution.py
+++ b/solution.py
@@ -18,12 +18,24 @@
     )
 
 
+def halves(a):
+    high = a.astype(jnp.bfloat16)
+    return high, (a - high.astype(F32)).astype(jnp.bfloat16)
+
+
+def dot3(a, b, ca, cb):
+    ah, al = halves(a)
+    bh, bl = halves(b)
+    one = lambda x, y: lax.dot_general(x, y, (((ca,), (cb,)), ((), ())), preferred_element_type=F32)
+    return one(ah, bh) + (one(ah, bl) + one(al, bh))
+
+
 def vmem(n):
     return [pl.BlockSpec(memory_space=pltpu.VMEM)] * n
 
 
 def hbm(n):
-    return [pl.BlockSpec(memory_space=pl.ANY)] * n
+    return [pl.BlockSpec(memory_space=pltpu.HBM)] * n
 
 
 class Place:
@@ -318,67 +330,107 @@
     for g in range(F):
         for h in range(parts):
             bp[g, h] = back[g * piece + h * sub:g * piece + (h + 1) * sub, :]
-    greet([{"replica": rx}, {"replica": ry}] + [at.line(d)[1] for d in range(1, F)] + tens)
-
-    sent = []
-
-    def go(copy):
-        copy.start()
-        sent.append(copy)
-
-    for h in range(parts):
-        for d in range(1, F):
-            q, where = at.line(d)
-            go(remote(bp.at[q, h], zrecv.at[at.f, h], z_send.at[h, d], z_recv.at[h, at.f], where))
-
-    def share_out(h, i):
-        g = at.line_from(i)
+    above, below = lax.rem(at.f + 1, F), lax.rem(at.f + F - 1, F)
+    sides = ({"fsdp": above}, {"fsdp": below})
+    greet([{"replica": rx}, {"replica": ry}] + list(sides) + tens)
+
+    started = []
+
+    def go(make, cond=None):
+        started.append((make, cond))
+        make().start()
+
+    def partial(e, g, h):
+        return remote(bp.at[g, h], zrecv.at[e, g, h], z_send.at[g, h], z_recv.at[e, g, h], sides[e])
+
+    for s in range(F - 1):
+        for h in range(parts):
+            for e, g in enumerate((F - 1 - s, s)):
+                cond = (at.f < g, at.f > g)[e]
+                inner = (cond & (at.f > 0), cond & (at.f < F - 1))[e]
+                make = lambda e=e, g=g, h=h: partial(e, g, h)
+                @pl.when(inner)
+                def _():
+                    make().wait_recv()
+                    bp[g, h] = bp[g, h] + zrecv[e, g, h]
+                @pl.when(cond)
+                def _():
+                    go(make, cond)
+
+    def pass_on(e, g, h):
         slot = full.at[at.r, g, h]
-        for e, k in enumerate((rx, ry)):
-            go(remote(slot, slot, r_send.at[h, i, e], r_recv.at[at.r, g, h], {"replica": k}))
+        return remote(slot, slot, a_send.at[e, g, h], a_recv.at[g, h], sides[e])
+
+    def share(e, g, h):
+        slot = full.at[at.r, g, h]
+        return remote(slot, slot, r_send.at[g, h, e], r_recv.at[at.r, g, h], {"replica": (rx, ry)[e]})
 
     def arrive(k, g, h):
         slot = full.at[k, g, h]
-        remote(slot, slot, r_send.at[h, 0, 0], r_recv.at[k, g, h], {"replica": rx}).wait_recv()
-
-    def cross_on(h, i):
-        g = at.line_from(i)
+        remote(slot, slot, r_send.at[g, h, 0], r_recv.at[k, g, h], {"replica": rx}).wait_recv()
+
+    def cross(g, h):
         odd = lax.rem(g, 2)
+        src = rx + (ry - rx) * odd
+        slot = full.at[src, g, h]
+        return remote(slot, slot, x_send.at[g, h], r_recv.at[src, g, h], {"replica": ry + (rx - ry) * odd})
+
+    def cross_on(g, h, cond):
         arrive(rx, g, h)
         arrive(ry, g, h)
-        src = rx + (ry - rx) * odd
-        dst = ry + (rx - ry) * odd
-        slot = full.at[src, g, h]
-        go(remote(slot, slot, x_send.at[h, i], r_recv.at[src, g, h], {"replica": dst}))
-
+        go(lambda: cross(g, h), cond)
+
+    more = (at.f < F - 1, at.f > 0)
     for h in range(parts):
-        zrecv[at.f, h] = bp[at.f, h]
-        for d in range(1, F):
-            q = at.line_from(d)
-            remote(bp.at[q, h], zrecv.at[q, h], z_send.at[h, d], z_recv.at[h, q], at.line(d)[1]).wait_recv()
-        total = zrecv[0, h]
-        for k in range(1, F):
-            total = total + zrecv[k, h]
-        full[at.r, at.f, h] = total
-        slot = full.at[at.r, at.f, h]
-        for d in range(1, F):
-            q, where = at.line(d)
-            go(remote(slot, slot, a_send.at[h, d], a_recv.at[h, at.f], where))
-        share_out(h, 0)
-    order = [(h, i) for h in range(parts) for i in range(1, F)]
-    late = [(h, 0) for h in range(parts)]
-    for h, i in order:
-        q = at.line_from(i)
-        slot = full.at[at.r, q, h]
-        remote(slot, slot, a_send.at[h, i], a_recv.at[h, q], at.line(i)[1]).wait_recv()
-        share_out(h, i)
-        late.append((h, i))
-        cross_on(*late.pop(0))
-    for h, i in late:
-        cross_on(h, i)
-    for h in range(parts):
-        for i in range(F):
-            arrive(rd, at.line_from(i), h)
+        @pl.when(at.f > 0)
+        def _():
+            partial(0, at.f, h).wait_recv()
+            bp[at.f, h] = bp[at.f, h] + zrecv[0, at.f, h]
+        @pl.when(at.f < F - 1)
+        def _():
+            partial(1, at.f, h).wait_recv()
+            bp[at.f, h] = bp[at.f, h] + zrecv[1, at.f, h]
+        full[at.r, at.f, h] = bp[at.f, h]
+        for e in range(2):
+            @pl.when(more[e])
+            def _():
+                go(lambda e=e, h=h: pass_on(e, at.f, h), more[e])
+        for e in range(2):
+            go(lambda e=e, h=h: share(e, at.f, h))
+    late = [(at.f, h, None) for h in range(parts)]
+    for s in range(1, F):
+        now = []
+        for h in range(parts):
+            for e in range(2):
+                g = (at.f - s, at.f + s)[e]
+                cond = (at.f >= s, at.f < F - s)[e]
+                both = cond & more[e]
+                @pl.when(cond)
+                def _():
+                    pass_on(e, g, h).wait_recv()
+                @pl.when(both)
+                def _():
+                    go(lambda e=e, g=g, h=h: pass_on(e, g, h), both)
+                @pl.when(cond)
+                def _():
+                    for i in range(2):
+                        go(lambda i=i, g=g, h=h: share(i, g, h), cond)
+                now.append((g, h, cond))
+        for g, h, cond in late:
+            if cond is None:
+                cross_on(g, h, None)
+            else:
+                @pl.when(cond)
+                def _():
+                    cross_on(g, h, cond)
+        late = now
+    for g, h, cond in late:
+        @pl.when(cond)
+        def _():
+            cross_on(g, h, cond)
+    for g in range(F):
+        for h in range(parts):
+            arrive(rd, g, h)
 
     squares = jnp.zeros((1, rank), F32)
     for k in range(R):
@@ -388,7 +440,7 @@
                 squares = squares + jnp.sum(v * v, axis=0, keepdims=True)
     sq[...] = jnp.broadcast_to(squares, sq.shape)
     for d in range(1, T):
-        go(remote(sq, sqrecv.at[at.t], s_send.at[d], s_recv.at[at.t], tens[d - 1]))
+        go(lambda d=d: remote(sq, sqrecv.at[at.t], s_send.at[d], s_recv.at[at.t], tens[d - 1]))
     sqrecv[at.t] = sq[...]
 
     for copy in loads:
@@ -400,7 +452,7 @@
             [full[k, g, h] for k in range(m * R // 2, (m + 1) * R // 2) for g in range(F) for h in range(parts)], axis=0
         )
         here = pl.ds(m * (cols // 2), cols // 2)
-        mom[:, here] = mom[:, here] + grad[:, here].astype(F32) + dot(o, block, 1, 1)
+        mom[:, here] = mom[:, here] + grad[:, here].astype(F32) + dot3(o, block, 1, 1)
         copy = pltpu.make_async_copy(mom.at[:, here], mom_out.at[0, :, here], out_sem.at[m])
         copy.start()
         stores.append(copy)
@@ -420,8 +472,13 @@
             right_out[first:first + sub, :] = full[k // F, lax.rem(k, F), h] * scale
     for copy in stores:
         copy.wait()
-    for copy in sent:
-        copy.wait_send()
+    for make, cond in started:
+        if cond is None:
+            make().wait_send()
+        else:
+            @pl.when(cond)
+            def _():
+                make().wait_send()
 
 
 def solution(mesh):
@@ -434,7 +491,7 @@
         qb, rank = right_in.shape
         share = cols // R
         nb = F // R
-        nc = 4 if qb % 32 == 0 else 1
+        nc = 8 if qb % 64 == 0 else 1
         piece = share // F
         parts = 2
         sds = jax.ShapeDtypeStruct
@@ -462,7 +519,7 @@
                 DMA((F,)), DMA((F,)), DMA((n,)), DMA((n,)),
             ],
             compiler_params=pltpu.CompilerParams(
-                collective_id=0, has_side_effects=True, vmem_limit_bytes=40 << 20
+                collective_id=0, has_side_effects=True, vmem_limit_bytes=60 << 20
             ),
             name="project",
         )(momentum, gradient, right_in)
@@ -472,7 +529,7 @@
             in_specs=vmem(2),
             out_specs=tuple(vmem(2)),
             scratch_shapes=[pltpu.VMEM((rank, 2 * rank), F32)],
-            compiler_params=pltpu.CompilerParams(vmem_limit_bytes=40 << 20),
+            compiler_params=pltpu.CompilerParams(vmem_limit_bytes=60 << 20),
             name="factor",
         )(gram, proj)
         right, updated = pl.pallas_call(
@@ -484,16 +541,16 @@
                 pltpu.VMEM((rows, cols), F32),
                 pltpu.VMEM((rows, cols), gradient.dtype),
                 pltpu.VMEM((F, parts, piece // parts, rank), F32),
-                pltpu.VMEM((F, parts, piece // parts, rank), F32),
+                pltpu.VMEM((2, F, parts, piece // parts, rank), F32),
                 pltpu.VMEM((R, F, parts, piece // parts, rank), F32),
                 pltpu.VMEM((8, rank), F32),
                 slots(T, 8),
                 DMA((2,)), DMA((2,)),
-                DMA((parts, F)), DMA((parts, F)), DMA((parts, F)), DMA((parts, F)),
-                DMA((parts, F, 2)), DMA((R, F, parts)), DMA((parts, F)), DMA((T,)), DMA((T,)),
+                DMA((F, parts)), DMA((2, F, parts)), DMA((2, F, parts)), DMA((F, parts)),
+                DMA((F, parts, 2)), DMA((R, F, parts)), DMA((F, parts)), DMA((T,)), DMA((T,)),
             ],
             compiler_params=pltpu.CompilerParams(
-                collective_id=1, has_side_effects=True, vmem_limit_bytes=40 << 20
+                collective_id=1, has_side_effects=True, vmem_limit_bytes=60 << 20
             ),
             name="back",
         )(momentum, gradient, bmean, ortho)

time: 107 us -> 115 us (1.075)
  the two profiles are of different devices: /device:TPU:17 before, /device:TPU:0 now
where the time goes in v3:
time: 115 us; the launch traced here: 114 us
  Pallas kernels  109 us (95%)
  local copies, waits for them, and re-layouts  4.66 us (4%)
    pallas_call x1, Pallas kernels, shards(): pl.pallas_call(lambda *refs: project_kernel(R, F, T, *refs), out_shape=(s...  49.7 us
    pallas_call x1, Pallas kernels, shards(): pl.pallas_call(lambda *refs: back_kernel(R, F, T, *refs), out_shape=(sds(...  47.2 us
    pallas_call x1, Pallas kernels, shards(): pl.pallas_call(lambda *refs: factor_kernel(math.sqrt(rows * F), *refs), o...  12.1 us
    unnamed x2, local copies, waits for them, and re-layouts  4.66 us

profile of v3, /device:TPU:0, one launch (start us, length us, event | category | flops | bytes accessed | tf_op | source)
XLA Modules:
  0.0 114.3 jit_solution(18414681243959247161)
XLA Ops:
  0.6 49.7 %project.1 = (f32[256,448]{1,0:T(8,128)}, f32[256,256]{1,0:T(8,128)}, f32[256,256]{1,0:T(8,128)}) custom-call(f32[1,256,1792]{2,1,0:T(8,128)} %refs_0_.3, bf16[1,256,1792]{2,1,0:T(8,128)(2,1)} %refs_1_.3, f32[448,256]{1,0:T(8,128)} %refs_2_.1), custom_call_target="tpu_custom_call" | custom-call | tf_op jit(solution)/shard_map/project/pallas_call | solution.py:499
  50.3 12.1 %factor.1 = (f32[256,256]{1,0:T(8,128)}, f32[256,256]{1,0:T(8,128)}) custom-call(f32[256,256]{1,0:T(8,128)} %get-tuple-element.10.refs_0_, f32[256,256]{1,0:T(8,128)} %get-tuple-element.11.refs_1_), custom_call_target="tpu_custom_call" | custom-call | tf_op jit(solution)/shard_map/factor/pallas_call | solution.py:526
  62.5 47.2 %back.1 = (f32[448,256]{1,0:T(8,128)}, f32[1,256,1792]{2,1,0:T(8,128)}) custom-call(f32[1,256,1792]{2,1,0:T(8,128)} %refs_0_.3, bf16[1,256,1792]{2,1,0:T(8,128)(2,1)} %refs_1_.3, f32[256,448]{1,0:T(8,128)} %get-tuple-element.13.refs_2_, f32[256,256]{1,0:T(8,128)} %get-tuple-element.14.refs_3_), custom_call_target="tpu_custom_call" | custom-call | tf_op jit(solution)/shard_map/back/pallas_call | solution.py:535
  109.6 1.8 %copy.8 = f32[448,256]{1,0:T(8,128)} copy(f32[448,256]{1,0:T(8,128)} %get-tuple-element.21) | data formatting | bytes 917504
  111.4 2.8 %copy.9 = f32[1,256,1792]{2,1,0:T(8,128)} copy(f32[1,256,1792]{2,1,0:T(8,128)} %get-tuple-element.22) | data formatting | bytes 3670016

commit v4 on v2

v4 whole, which is shorter than its diff:
```python
import math

import jax
import jax.numpy as jnp
from jax import lax
from jax.experimental import pallas as pl
from jax.experimental.pallas import tpu as pltpu
from jax.sharding import PartitionSpec as P

MESH = pl.DeviceIdType.MESH
HIGHEST = lax.Precision.HIGHEST
F32 = jnp.float32


def dot(a, b, ca, cb):
    return lax.dot_general(
        a, b, (((ca,), (cb,)), ((), ())), precision=HIGHEST, preferred_element_type=F32
    )


def halves(a):
    high = a.astype(jnp.bfloat16)
    return high, (a - high.astype(F32)).astype(jnp.bfloat16)


def dot3(a, b, ca, cb):
    ah, al = halves(a)
    bh, bl = halves(b)
    one = lambda x, y: lax.dot_general(x, y, (((ca,), (cb,)), ((), ())), preferred_element_type=F32)
    return one(ah, bh) + (one(ah, bl) + one(al, bh))


def vmem(n):
    return [pl.BlockSpec(memory_space=pltpu.VMEM)] * n


def hbm(n):
    return [pl.BlockSpec(memory_space=pltpu.HBM)] * n


class Place:
    def __init__(self, R, F, T):
        self.R, self.F, self.T, self.n = R, F, T, R * T
        self.r = lax.axis_index("replica")
        self.f = lax.axis_index("fsdp")
        self.t = lax.axis_index("tensor")
        self.p = self.r * T + self.t

    def plane(self, d):
        q = lax.rem(self.p + d, self.n)
        return q, {"replica": q // self.T, "tensor": lax.rem(q, self.T)}

    def plane_from(self, d):
        return lax.rem(self.p + self.n - d, self.n)

    def line(self, d):
        q = lax.rem(self.f + d, self.F)
        return q, {"fsdp": q}

    def line_from(self, d):
        return lax.rem(self.f + self.F - d, self.F)

    def cross(self):
        low = lax.rem(self.r, 2)
        return self.r + 1 - 2 * low, lax.rem(self.r + 2, 4), 3 - self.r

    def rep(self, d):
        q = lax.rem(self.r + d, self.R)
        return q, {"replica": q}

    def rep_from(self, d):
        return lax.rem(self.r + self.R - d, self.R)


def remote(src, dst, send, recv, where):
    return pltpu.make_async_remote_copy(
        src_ref=src, dst_ref=dst, send_sem=send, recv_sem=recv, device_id=where, device_id_type=MESH
    )


def greet(targets):
    barrier = pltpu.get_barrier_semaphore()
    for where in targets:
        pl.semaphore_signal(barrier, inc=1, device_id=where, device_id_type=MESH)
    pl.semaphore_wait(barrier, len(targets))


def pack(part):
    rows, share = part.shape
    whole = share // 128 * 128
    tiles = [part[:, i:i + 128] for i in range(0, whole, 128)]
    if whole < share:
        half = rows // 2
        tiles.append(jnp.concatenate([part[:half, whole:], part[half:, whole:]], axis=1))
    return jnp.concatenate(tiles, axis=0)


def unpack(flat, rows, share):
    whole = share // 128 * 128
    tiles = [flat[i * rows:(i + 1) * rows] for i in range(whole // 128)]
    if whole < share:
        last = flat[whole // 128 * rows:]
        tiles.append(jnp.concatenate([last[:, :64], last[:, 64:]], axis=0))
    return jnp.concatenate(tiles, axis=1)


def project_kernel(
    R, F, T, mom_in, grad_in, q_in, bmean_out, proj_out,
    mom, grad, bufs, brecv, qs, pp, precv, proj,
    in_sem, q_sem, b_send, b_recv, q_up, q_down, q_recv, p_send, p_recv, a_send, a_recv,
):
    at = Place(R, F, T)
    rows, cols = mom.shape
    share = cols // R
    n = at.n
    loads = [
        pltpu.make_async_copy(mom_in.at[0], mom, in_sem.at[0]),
        pltpu.make_async_copy(grad_in.at[0], grad, in_sem.at[1]),
    ]
    for copy in loads:
        copy.start()
    nb = F // R
    nc, qc = qs.shape[1], qs.shape[2]

    def fetch(j, c):
        return pltpu.make_async_copy(q_in.at[pl.ds(c * qc, qc)], qs.at[j, c], q_sem.at[j, c])

    for j in range(nb):
        @pl.when(at.f == at.r * nb + j)
        def _():
            for c in range(nc):
                fetch(j, c).start()

    greet([at.plane(d)[1] for d in range(1, n)] + [at.line(d)[1] for d in range(1, F)])

    for copy in loads:
        copy.wait()
    half = bufs.shape[2]
    for k in range(R):
        part = slice(k * share, (k + 1) * share)
        flat = pack(mom[:, part] + grad[:, part].astype(F32))
        for h in range(2):
            bufs[k, h] = flat[h * half:(h + 1) * half]

    rx, ry, rd = at.cross()
    sent = []

    def hop(src, h, slot, k):
        return remote(bufs.at[src, h], brecv.at[h, slot], b_send.at[h, slot], b_recv.at[h, slot], {"replica": k})

    for slot in range(2):
        for h, first in enumerate((rx, ry)):
            copy = hop((rd, first)[slot], h, slot, first)
            copy.start()
            sent.append(copy)

    def up(j, c):
        return remote(qs.at[j, c], qs.at[j, c], q_up.at[j, c], q_recv.at[j, c], {"fsdp": lax.rem(at.f + 1, F)})

    def down(j, c):
        return remote(qs.at[j, c], qs.at[j, c], q_down.at[j, c], q_recv.at[j, c], {"fsdp": lax.rem(at.f + F - 1, F)})

    def pass_on(c, j):
        home = at.r * nb + j
        @pl.when(at.f == home)
        def _():
            fetch(j, c).wait()
        @pl.when(at.f != home)
        def _():
            up(j, c).wait_recv()
        @pl.when((at.f >= home) & (at.f < F - 1))
        def _():
            up(j, c).start()
        @pl.when((at.f <= home) & (at.f > 0))
        def _():
            down(j, c).start()

    for c in range(nc):
        for j in range(nb):
            pass_on(c, j)
        if c == 0:
            for h, second in enumerate((ry, rx)):
                hop(rd, h, 0, second).wait_recv()
                bufs[second, h] = bufs[second, h] + brecv[h, 0]
                copy = hop(second, h, 2, second)
                copy.start()
                sent.append(copy)
    for h, (first, second) in enumerate(((rx, ry), (ry, rx))):
        hop(first, h, 1, first).wait_recv()
    for h, second in enumerate((ry, rx)):
        hop(second, h, 2, second).wait_recv()
    flat = jnp.concatenate([bufs[at.r, h] + brecv[h, 1] + brecv[h, 2] for h in range(2)], axis=0)
    bmean = unpack(flat * (1.0 / R), rows, share)
    bmean_out[...] = bmean
    part = dot(bmean, qs[...].reshape(share, q_in.shape[1]), 1, 0)
    pp[...] = part.reshape(pp.shape)

    for d in range(1, n):
        q, where = at.plane(d)
        copy = remote(pp.at[q], precv.at[at.p], p_send.at[d - 1], p_recv.at[at.p], where)
        copy.start()
        sent.append(copy)
    precv[at.p] = pp[at.p]
    for d in range(1, n):
        q = at.plane_from(d)
        remote(pp.at[q], precv.at[q], p_send.at[d - 1], p_recv.at[q], at.plane(d)[1]).wait_recv()
    total = precv[0]
    for k in range(1, n):
        total = total + precv[k]
    proj[at.p] = total
    for d in range(1, n):
        q, where = at.plane(d)
        copy = remote(proj.at[at.p], proj.at[at.p], a_send.at[d - 1], a_recv.at[at.p], where)
        copy.start()
        sent.append(copy)
    for d in range(1, n):
        q = at.plane_from(d)
        remote(proj.at[q], proj.at[q], a_send.at[d - 1], a_recv.at[q], at.plane(d)[1]).wait_recv()
    whole = proj[...].reshape(rows, q_in.shape[1])
    proj_out[...] = whole

    for copy in sent:
        copy.wait_send()
    for c in range(nc):
        for j in range(nb):
            home = at.r * nb + j
            @pl.when((at.f >= home) & (at.f < F - 1))
            def _():
                up(j, c).wait_send()
            @pl.when((at.f <= home) & (at.f > 0))
            def _():
                down(j, c).wait_send()


def eliminate(tile, side):
    b = tile.shape[0]
    rows_id = lax.broadcasted_iota(jnp.int32, tile.shape, 0)
    lanes = lax.broadcasted_iota(jnp.int32, tile.shape, 1)
    other = b - side
    inside = (lanes >= side) & (lanes < side + b)
    x = jnp.where(inside, tile, jnp.where(lanes - other == rows_id, 1.0, 0.0).astype(F32))
    done = []
    for k0 in range(0, b, 8):
        shape = x.shape
        ids = lax.broadcasted_iota(jnp.int32, shape, 0)
        panel = [
            jnp.broadcast_to(x[:, side + k0 + j:side + k0 + j + 1], shape) for j in range(8)
        ]
        for j in range(8):
            inverse = 1.0 / panel[j][j:j + 1, :]
            scale = jnp.where(ids > j, panel[j], 0.0) * inverse
            for i in range(j + 1, 8):
                panel[i] = panel[i] - scale * panel[i][j:j + 1, :]
            x = x - scale * x[j:j + 1, :]
        done.append(x[:8])
        x = x[8:]
    x = jnp.concatenate(done, axis=0)
    pivot = jnp.sum(jnp.where(lanes - side == rows_id, x, 0.0), axis=1, keepdims=True)
    return x * (1.0 / jnp.sqrt(pivot))


def factor_step(w, o, b):
    size = w.shape[0]
    base = o // 128 * 128
    side = o - base
    x = eliminate(w[o:o + b, base:base + 128], side)
    block = w[o:o + b, :]
    zero = jnp.zeros_like(block)
    stack = jnp.concatenate([zero, block] if side == 0 else [block, zero], axis=0)
    strip = dot(x, stack, 1, 0)
    w[o:o + b, :] = strip
    if o + b < size:
        update = dot(strip[:, :size], strip, 0, 0)
        w[o + b:, :] = w[o + b:, :] - update[o + b:, :]


def back_kernel(
    R, F, T, mom_in, grad_in, bmean, proj, left_out, right_out, mom_out,
    mom, grad, gp, grecv, gram, w, bp, zrecv, full, sq, sqrecv,
    in_sem, g_send, g_recv, h_send, h_recv,
    z_send, z_recv, a_send, a_recv, r_send, r_recv, s_send, s_recv,
):
    at = Place(R, F, T)
    n = at.n
    loads = [
        pltpu.make_async_copy(mom_in.at[0], mom, in_sem.at[0]),
        pltpu.make_async_copy(grad_in.at[0], grad, in_sem.at[1]),
    ]
    for copy in loads:
        copy.start()
    rows, cols = mom.shape
    piece = bp.shape[1]
    rank = proj.shape[1]
    tens = [{"tensor": lax.rem(at.t + d, T)} for d in range(1, T)]
    sent = []

    def go(copy):
        copy.start()
        sent.append(copy)

    whole = proj[...]
    gp[...] = dot(whole, whole, 0, 0).reshape(gp.shape)
    greet([at.plane(d)[1] for d in range(1, n)] + [at.line(d)[1] for d in range(1, F)])
    for d in range(1, F):
        q, where = at.line(d)
        go(remote(gp.at[at.p], grecv.at[at.f], g_send.at[d - 1], g_recv.at[at.f], where))
    grecv[at.f] = gp[at.p]

    back = dot(bmean[...], whole, 0, 0)
    for g in range(F):
        bp[g] = back[g * piece:(g + 1) * piece, :]
    for d in range(1, F):
        q, where = at.line(d)
        go(remote(bp.at[q], zrecv.at[at.f], z_send.at[d - 1], z_recv.at[at.f], where))
    zrecv[at.f] = bp[at.f]

    for d in range(1, F):
        q = at.line_from(d)
        remote(gp.at[at.p], grecv.at[q], g_send.at[d - 1], g_recv.at[q], at.line(d)[1]).wait_recv()
    total = grecv[0]
    for k in range(1, F):
        total = total + grecv[k]
    gram[at.p] = total
    for d in range(1, n):
        q, where = at.plane(d)
        go(remote(gram.at[at.p], gram.at[at.p], h_send.at[d - 1], h_recv.at[at.p], where))
    for d in range(1, n):
        q = at.plane_from(d)
        remote(gram.at[q], gram.at[q], h_send.at[d - 1], h_recv.at[q], at.plane(d)[1]).wait_recv()
    w[:, :rank] = gram[...].reshape(rank, rank)
    ids = lax.broadcasted_iota(jnp.int32, (rank, rank), 0)
    lanes = lax.broadcasted_iota(jnp.int32, (rank, rank), 1)
    w[:, rank:] = jnp.where(ids == lanes, 1.0, 0.0).astype(F32)

    def forward(f, i):
        for d in range(1, R):
            q, where = at.rep(d)
            go(remote(full.at[at.r, f], full.at[at.r, f], r_send.at[i, d - 1], r_recv.at[at.r, f], where))

    def reduced():
        for d in range(1, F):
            q = at.line_from(d)
            remote(bp.at[q], zrecv.at[q], z_send.at[d - 1], z_recv.at[q], at.line(d)[1]).wait_recv()
        total = zrecv[0]
        for k in range(1, F):
            total = total + zrecv[k]
        full[at.r, at.f] = total
        for d in range(1, F):
            q, where = at.line(d)
            go(remote(full.at[at.r, at.f], full.at[at.r, at.f], a_send.at[d - 1], a_recv.at[at.f], where))
        forward(at.f, 0)

    def gathered(d):
        q = at.line_from(d)
        remote(full.at[at.r, q], full.at[at.r, q], a_send.at[d - 1], a_recv.at[q], at.line(d)[1]).wait_recv()
        forward(q, d)

    reduced()
    b = 64
    moves = [lambda d=d: gathered(d) for d in range(1, F)]
    steps = rank // b
    for i in range(steps):
        factor_step(w, i * b, b)
        due = len(moves) * (i + 1) // (steps - 1) - len(moves) * i // (steps - 1) if i < steps - 1 else 0
        first = len(moves) * i // (steps - 1)
        for m in moves[first:first + due]:
            m()
    inverse = w[:, rank:]
    ortho = dot(whole, inverse, 1, 1)
    left_out[...] = ortho * math.sqrt(rows * F)
    for i in range(F):
        g = at.line_from(i)
        for d in range(1, R):
            k = at.rep_from(d)
            remote(full.at[k, g], full.at[k, g], r_send.at[i, d - 1], r_recv.at[k, g], at.rep(d)[1]).wait_recv()
    for copy in sent:
        copy.wait_send()

    squares = jnp.zeros((1, rank), F32)
    blocks = []
    for m in range(2):
        terms = jnp.concatenate(
            [full[k, g] for k in range(m * R // 2, (m + 1) * R // 2) for g in range(F)], axis=0
        )
        v = dot(terms, inverse, 1, 1)
        squares = squares + jnp.sum(v * v, axis=0, keepdims=True)
        count = R * F // 2
        for i in range(count):
            j = m * count + i
            full[j // F, j % F] = v[i * piece:(i + 1) * piece]
        blocks.append(v)
    sq[...] = jnp.broadcast_to(squares, sq.shape)
    norms = []
    for d in range(1, T):
        copy = remote(sq, sqrecv.at[at.t], s_send.at[d - 1], s_recv.at[at.t], tens[d - 1])
        copy.start()
        norms.append(copy)
    sqrecv[at.t] = sq[...]

    for copy in loads:
        copy.wait()
    o = ortho * -0.1
    for m in range(2):
        here = pl.ds(m * (cols // 2), cols // 2)
        mom_out[0, :, here] = mom[:, here] + grad[:, here].astype(F32) + dot3(o, blocks[m], 1, 1)

    for d in range(1, T):
        k = lax.rem(at.t + T - d, T)
        remote(sq, sqrecv.at[k], s_send.at[d - 1], s_recv.at[k], tens[d - 1]).wait_recv()
    total = sqrecv[0]
    for k in range(1, T):
        total = total + sqrecv[k]
    norm = jnp.sqrt(total[0:1, :] + 1e-06)
    scale = math.sqrt(cols * T) / norm
    for i in range(R):
        k = at.f * R + i
        right_out[i * piece:(i + 1) * piece, :] = full[k // F, lax.rem(k, F)] * scale
    for copy in norms:
        copy.wait_send()


def solution(mesh):
    R, F, T = mesh.shape["replica"], mesh.shape["fsdp"], mesh.shape["tensor"]
    n = R * T
    DMA = pltpu.SemaphoreType.DMA

    def shards(momentum, gradient, right_in):
        rows, cols = momentum.shape[1], momentum.shape[2]
        qb, rank = right_in.shape
        share = cols // R
        nb = F // R
        nc = 8 if qb % 64 == 0 else 1
        piece = share // F
        sds = jax.ShapeDtypeStruct
        slots = lambda m, r: pltpu.VMEM((m, r, rank), F32)
        bmean, proj = pl.pallas_call(
            lambda *refs: project_kernel(R, F, T, *refs),
            out_shape=(sds((rows, share), F32), sds((rows, rank), F32)),
            in_specs=hbm(3),
            out_specs=tuple(vmem(2)),
            scratch_shapes=[
                pltpu.VMEM((rows, cols), F32),
                pltpu.VMEM((rows, cols), gradient.dtype),
                pltpu.VMEM((R, 2, rows * share // 256, 128), F32),
                pltpu.VMEM((2, 3, rows * share // 256, 128), F32),
                pltpu.VMEM((nb, nc, qb // nc, rank), F32),
                slots(n, rows // n),
                slots(n, rows // n),
                slots(n, rows // n),
                DMA((2,)), DMA((nb, nc)), DMA((2, 3)), DMA((2, 3)),
                DMA((nb, nc)), DMA((nb, nc)), DMA((nb, nc)),
                DMA((n,)), DMA((n,)), DMA((n,)), DMA((n,)),
            ],
            compiler_params=pltpu.CompilerParams(
                collective_id=0, has_side_effects=True, vmem_limit_bytes=60 << 20
            ),
            name="project",
        )(momentum, gradient, right_in)
        left, right, updated = pl.pallas_call(
            lambda *refs: back_kernel(R, F, T, *refs),
            out_shape=(sds((rows, rank), F32), sds((qb, rank), F32), sds(momentum.shape, F32)),
            in_specs=hbm(2) + vmem(2),
            out_specs=tuple(vmem(3)),
            scratch_shapes=[
                pltpu.VMEM((rows, cols), F32),
                pltpu.VMEM((rows, cols), gradient.dtype),
                slots(n, rank // n),
                slots(F, rank // n),
                slots(n, rank // n),
                pltpu.VMEM((rank, 2 * rank), F32),
                slots(F, piece),
                slots(F, piece),
                pltpu.VMEM((R, F, piece, rank), F32),
                pltpu.VMEM((8, rank), F32),
                slots(T, 8),
                DMA((2,)),
                DMA((F,)), DMA((F,)), DMA((n,)), DMA((n,)),
                DMA((F,)), DMA((F,)), DMA((F,)), DMA((F,)),
                DMA((F, R)), DMA((R, F)), DMA((T,)), DMA((T,)),
            ],
            compiler_params=pltpu.CompilerParams(
                collective_id=1, has_side_effects=True, vmem_limit_bytes=40 << 20
            ),
            name="back",
        )(momentum, gradient, bmean, proj)
        return left, right, updated

    placed = (
        P("replica", "fsdp", "tensor"),
        P("replica", "fsdp", "tensor"),
        P(("tensor", "fsdp"), None),
    )
    return jax.shard_map(
        shards,
        mesh=mesh,
        in_specs=placed,
        out_specs=(P("fsdp", None), P(("tensor", "fsdp"), None), P("replica", "fsdp", "tensor")),
        check_vma=False,
    )
```

time: 107 us -> 94.8 us (0.89); the launches traced: 105 us -> 94.6 us
  Pallas kernels: 98.3 us -> 89.3 us
    pallas_call x1, Pallas kernels: 39.1 us -> 54.9 us  [shards(): pl.pallas_call(lambda *refs: back_kernel(R, F, T, *refs), out_shape=(sds(...]
    pallas_call x1, Pallas kernels: 48.3 us -> 34.4 us  [shards(): pl.pallas_call(lambda *refs: project_kernel(R, F, T, *refs), out_shape=(s...]
    pallas_call x1 -> x0, Pallas kernels: 11 us -> none  [shards(): pl.pallas_call(lambda *refs: factor_kernel(math.sqrt(rows * F), *refs), o...]
    unnamed x10 -> x11, local copies, waits for them, and re-layouts: 5.69 us -> 4.69 us
where the time goes in v4:
time: 94.8 us; the launch traced here: 94.6 us
  Pallas kernels  89.3 us (94%)
  local copies, waits for them, and re-layouts  4.69 us (5%)
    pallas_call x1, Pallas kernels, shards(): pl.pallas_call(lambda *refs: back_kernel(R, F, T, *refs), out_shape=(sds(...  54.9 us
    pallas_call x1, Pallas kernels, shards(): pl.pallas_call(lambda *refs: project_kernel(R, F, T, *refs), out_shape=(s...  34.4 us
    unnamed x11, local copies, waits for them, and re-layouts  4.69 us

profile of v4, /device:TPU:17, one launch (start us, length us, event | category | flops | bytes accessed | tf_op | source)
XLA Modules:
  0.0 94.6 jit_solution(12509081962582382824)
XLA Ops:
  0.6 0.0 copy-start.1
  0.6 0.0 copy-start
  0.7 34.4 %project.1 = (f32[256,448]{1,0:T(8,128)}, f32[256,256]{1,0:T(8,128)}) custom-call(f32[1,256,1792]{2,1,0:T(8,128)} %refs_0_.3, bf16[1,256,1792]{2,1,0:T(8,128)(2,1)} %refs_1_.3, f32[448,256]{1,0:T(8,128)} %refs_2_.1), custom_call_target="tpu_custom_call" | custom-call | tf_op jit(solution)/shard_map/project/pallas_call | solution.py:436
  35.0 0.0 copy-done.1
  35.0 0.0 copy-done
  35.1 0.0 copy-start.2
  35.1 1.0 %copy-done.2 = f32[256,448]{1,0:T(8,128)S(1)} copy-done((f32[256,448]{1,0:T(8,128)S(1)}, f32[256,448]{1,0:T(8,128)}, u32[]{:S(2)}) %copy-start.2) | copy-done | bytes 458776
  36.1 0.0 copy-start.3
  36.1 0.9 %copy-done.3 = f32[256,256]{1,0:T(8,128)S(1)} copy-done((f32[256,256]{1,0:T(8,128)S(1)}, f32[256,256]{1,0:T(8,128)}, u32[]{:S(2)}) %copy-start.3) | copy-done | bytes 262168
  37.1 54.9 %back.1 = (f32[256,256]{1,0:T(8,128)S(1)}, f32[448,256]{1,0:T(8,128)S(1)}, f32[1,256,1792]{2,1,0:T(8,128)S(1)}) custom-call(f32[1,256,1792]{2,1,0:T(8,128)S(1)} %copy-done, bf16[1,256,1792]{2,1,0:T(8,128)(2,1)S(1)} %copy-done.1, f32[256,448]{1,0:T(8,128)S(1)} %copy-done.2, f32[256,256]{1,0:T(8,128)S(1)} %copy-done.3), custom_call_target="tpu_custom_call" | custom-call | tf_op jit(solution)/shard_map/back/pallas_call | solution.py:459
  91.9 0.7 copy.9
  92.6 0.8 copy.10
  93.4 1.2 %copy.11 = f32[1,256,1792]{2,1,0:T(8,128)} copy(f32[1,256,1792]{2,1,0:T(8,128)S(1)} %get-tuple-element.12) | data formatting | bytes 3670016
Async XLA Ops:
  0.6 34.4 %copy-start.1 = (bf16[1,256,1792]{2,1,0:T(8,128)(2,1)S(1)}, bf16[1,256,1792]{2,1,0:T(8,128)(2,1)}, u32[]{:S(2)}) copy-start(bf16[1,256,1792]{2,1,0:T(8,128)(2,1)} %refs_1_.3) | copy-start | bytes 2752516
  0.6 34.4 %copy-start = (f32[1,256,1792]{2,1,0:T(8,128)S(1)}, f32[1,256,1792]{2,1,0:T(8,128)}, u32[]{:S(2)}) copy-start(f32[1,256,1792]{2,1,0:T(8,128)} %refs_0_.3) | copy-start | bytes 5505028
  35.1 1.0 %copy-start.2 = (f32[256,448]{1,0:T(8,128)S(1)}, f32[256,448]{1,0:T(8,128)}, u32[]{:S(2)}) copy-start(f32[256,448]{1,0:T(8,128)} %get-tuple-element.5.refs_2_) | copy-start | bytes 1376260
  36.1 0.9 %copy-start.3 = (f32[256,256]{1,0:T(8,128)S(1)}, f32[256,256]{1,0:T(8,128)}, u32[]{:S(2)}) copy-start(f32[256,256]{1,0:T(8,128)} %get-tuple-element.6.refs_3_) | copy-start | bytes 786436

commit v5 on v4

--- a/solution.py
+++ b/solution.py
@@ -276,7 +276,7 @@
 
 def back_kernel(
     R, F, T, mom_in, grad_in, bmean, proj, left_out, right_out, mom_out,
-    mom, grad, gp, grecv, gram, w, bp, zrecv, full, sq, sqrecv,
+    mom, grad, gp, grecv, gram, w, bp, zrecv, full, final, sq, sqrecv,
     in_sem, g_send, g_recv, h_send, h_recv,
     z_send, z_recv, a_send, a_recv, r_send, r_recv, s_send, s_recv,
 ):
@@ -300,15 +300,15 @@
 
     whole = proj[...]
     gp[...] = dot(whole, whole, 0, 0).reshape(gp.shape)
+    back = dot(bmean[...], whole, 0, 0)
+    for g in range(F):
+        bp[g] = back[g * piece:(g + 1) * piece, :]
     greet([at.plane(d)[1] for d in range(1, n)] + [at.line(d)[1] for d in range(1, F)])
     for d in range(1, F):
         q, where = at.line(d)
         go(remote(gp.at[at.p], grecv.at[at.f], g_send.at[d - 1], g_recv.at[at.f], where))
     grecv[at.f] = gp[at.p]
 
-    back = dot(bmean[...], whole, 0, 0)
-    for g in range(F):
-        bp[g] = back[g * piece:(g + 1) * piece, :]
     for d in range(1, F):
         q, where = at.line(d)
         go(remote(bp.at[q], zrecv.at[at.f], z_send.at[d - 1], z_recv.at[at.f], where))
@@ -324,13 +324,6 @@
     for d in range(1, n):
         q, where = at.plane(d)
         go(remote(gram.at[at.p], gram.at[at.p], h_send.at[d - 1], h_recv.at[at.p], where))
-    for d in range(1, n):
-        q = at.plane_from(d)
-        remote(gram.at[q], gram.at[q], h_send.at[d - 1], h_recv.at[q], at.plane(d)[1]).wait_recv()
-    w[:, :rank] = gram[...].reshape(rank, rank)
-    ids = lax.broadcasted_iota(jnp.int32, (rank, rank), 0)
-    lanes = lax.broadcasted_iota(jnp.int32, (rank, rank), 1)
-    w[:, rank:] = jnp.where(ids == lanes, 1.0, 0.0).astype(F32)
 
     def forward(f, i):
         for d in range(1, R):
@@ -356,39 +349,37 @@
         forward(q, d)
 
     reduced()
+    for d in range(1, n):
+        q = at.plane_from(d)
+        remote(gram.at[q], gram.at[q], h_send.at[d - 1], h_recv.at[q], at.plane(d)[1]).wait_recv()
+    w[:, :rank] = gram[...].reshape(rank, rank)
+    ids = lax.broadcasted_iota(jnp.int32, (rank, rank), 0)
+    lanes = lax.broadcasted_iota(jnp.int32, (rank, rank), 1)
+    w[:, rank:] = jnp.where(ids == lanes, 1.0, 0.0).astype(F32)
     b = 64
-    moves = [lambda d=d: gathered(d) for d in range(1, F)]
     steps = rank // b
+    later = steps // 2
+    moved = 1
     for i in range(steps):
         factor_step(w, i * b, b)
-        due = len(moves) * (i + 1) // (steps - 1) - len(moves) * i // (steps - 1) if i < steps - 1 else 0
-        first = len(moves) * i // (steps - 1)
-        for m in moves[first:first + due]:
-            m()
+        if later <= i + 1 < steps:
+            until = F if i + 2 == steps else moved + max(1, (F - 1) // (steps - later))
+            for d in range(moved, min(until, F)):
+                gathered(d)
+            moved = min(until, F)
     inverse = w[:, rank:]
     ortho = dot(whole, inverse, 1, 1)
     left_out[...] = ortho * math.sqrt(rows * F)
+    squares = jnp.zeros((1, rank), F32)
     for i in range(F):
         g = at.line_from(i)
         for d in range(1, R):
             k = at.rep_from(d)
             remote(full.at[k, g], full.at[k, g], r_send.at[i, d - 1], r_recv.at[k, g], at.rep(d)[1]).wait_recv()
-    for copy in sent:
-        copy.wait_send()
-
-    squares = jnp.zeros((1, rank), F32)
-    blocks = []
-    for m in range(2):
-        terms = jnp.concatenate(
-            [full[k, g] for k in range(m * R // 2, (m + 1) * R // 2) for g in range(F)], axis=0
-        )
-        v = dot(terms, inverse, 1, 1)
+        v = dot(jnp.concatenate([full[k, g] for k in range(R)], axis=0), inverse, 1, 1)
         squares = squares + jnp.sum(v * v, axis=0, keepdims=True)
-        count = R * F // 2
-        for i in range(count):
-            j = m * count + i
-            full[j // F, j % F] = v[i * piece:(i + 1) * piece]
-        blocks.append(v)
+        for k in range(R):
+            final[k, g] = v[k * piece:(k + 1) * piece]
     sq[...] = jnp.broadcast_to(squares, sq.shape)
     norms = []
     for d in range(1, T):
@@ -402,7 +393,10 @@
     o = ortho * -0.1
     for m in range(2):
         here = pl.ds(m * (cols // 2), cols // 2)
-        mom_out[0, :, here] = mom[:, here] + grad[:, here].astype(F32) + dot3(o, blocks[m], 1, 1)
+        block = jnp.concatenate(
+            [final[k, g] for k in range(m * R // 2, (m + 1) * R // 2) for g in range(F)], axis=0
+        )
+        mom_out[0, :, here] = mom[:, here] + grad[:, here].astype(F32) + dot3(o, block, 1, 1)
 
     for d in range(1, T):
         k = lax.rem(at.t + T - d, T)
@@ -414,8 +408,8 @@
     scale = math.sqrt(cols * T) / norm
     for i in range(R):
         k = at.f * R + i
-        right_out[i * piece:(i + 1) * piece, :] = full[k // F, lax.rem(k, F)] * scale
-    for copy in norms:
+        right_out[i * piece:(i + 1) * piece, :] = final[k // F, lax.rem(k, F)] * scale
+    for copy in sent + norms:
         copy.wait_send()
 
 
@@ -471,6 +465,7 @@
                 slots(F, piece),
                 slots(F, piece),
                 pltpu.VMEM((R, F, piece, rank), F32),
+                pltpu.VMEM((R, F, piece, rank), F32),
                 pltpu.VMEM((8, rank), F32),
                 slots(T, 8),
                 DMA((2,)),

time: 94.8 us -> 91.4 us (0.964)
  Pallas kernels: 89.3 us -> 85.8 us
    pallas_call x1, Pallas kernels: 54.9 us -> 51.4 us  [shards(): pl.pallas_call(lambda *refs: back_kernel(R, F, T, *refs), out_shape=(sds(...]
where the time goes in v5:
time: 91.4 us; the launch traced here: 91.2 us
  Pallas kernels  85.8 us (94%)
  local copies, waits for them, and re-layouts  4.69 us (5%)
    pallas_call x1, Pallas kernels, shards(): pl.pallas_call(lambda *refs: back_kernel(R, F, T, *refs), out_shape=(sds(...  51.4 us
    pallas_call x1, Pallas kernels, shards(): pl.pallas_call(lambda *refs: project_kernel(R, F, T, *refs), out_shape=(s...  34.4 us
    unnamed x11, local copies, waits for them, and re-layouts  4.69 us

profile of v5, /device:TPU:17, one launch (start us, length us, event | category | flops | bytes accessed | tf_op | source)
XLA Modules:
  0.0 91.2 jit_solution(1602089367345417362)
XLA Ops:
  0.6 0.0 copy-start.1
  0.6 0.0 copy-start
  0.7 34.4 %project.1 = (f32[256,448]{1,0:T(8,128)}, f32[256,256]{1,0:T(8,128)}) custom-call(f32[1,256,1792]{2,1,0:T(8,128)} %refs_0_.3, bf16[1,256,1792]{2,1,0:T(8,128)(2,1)} %refs_1_.3, f32[448,256]{1,0:T(8,128)} %refs_2_.1), custom_call_target="tpu_custom_call" | custom-call | tf_op jit(solution)/shard_map/project/pallas_call | solution.py:430
  35.0 0.0 copy-done.1
  35.0 0.0 copy-done
  35.1 0.0 copy-start.2
  35.1 1.0 %copy-done.2 = f32[256,448]{1,0:T(8,128)S(1)} copy-done((f32[256,448]{1,0:T(8,128)S(1)}, f32[256,448]{1,0:T(8,128)}, u32[]{:S(2)}) %copy-start.2) | copy-done | bytes 458776
  36.1 0.0 copy-start.3
  36.1 0.9 %copy-done.3 = f32[256,256]{1,0:T(8,128)S(1)} copy-done((f32[256,256]{1,0:T(8,128)S(1)}, f32[256,256]{1,0:T(8,128)}, u32[]{:S(2)}) %copy-start.3) | copy-done | bytes 262168
  37.1 51.4 %back.1 = (f32[256,256]{1,0:T(8,128)S(1)}, f32[448,256]{1,0:T(8,128)S(1)}, f32[1,256,1792]{2,1,0:T(8,128)S(1)}) custom-call(f32[1,256,1792]{2,1,0:T(8,128)S(1)} %copy-done, bf16[1,256,1792]{2,1,0:T(8,128)(2,1)S(1)} %copy-done.1, f32[256,448]{1,0:T(8,128)S(1)} %copy-done.2, f32[256,256]{1,0:T(8,128)S(1)} %copy-done.3), custom_call_target="tpu_custom_call" | custom-call | tf_op jit(solution)/shard_map/back/pallas_call | solution.py:453
  88.5 0.7 copy.9
  89.2 0.8 copy.10
  90.0 1.2 %copy.11 = f32[1,256,1792]{2,1,0:T(8,128)} copy(f32[1,256,1792]{2,1,0:T(8,128)S(1)} %get-tuple-element.12) | data formatting | bytes 3670016
Async XLA Ops:
  0.6 34.4 %copy-start.1 = (bf16[1,256,1792]{2,1,0:T(8,128)(2,1)S(1)}, bf16[1,256,1792]{2,1,0:T(8,128)(2,1)}, u32[]{:S(2)}) copy-start(bf16[1,256,1792]{2,1,0:T(8,128)(2,1)} %refs_1_.3) | copy-start | bytes 2752516
  0.6 34.4 %copy-start = (f32[1,256,1792]{2,1,0:T(8,128)S(1)}, f32[1,256,1792]{2,1,0:T(8,128)}, u32[]{:S(2)}) copy-start(f32[1,256,1792]{2,1,0:T(8,128)} %refs_0_.3) | copy-start | bytes 5505028
  35.1 1.0 %copy-start.2 = (f32[256,448]{1,0:T(8,128)S(1)}, f32[256,448]{1,0:T(8,128)}, u32[]{:S(2)}) copy-start(f32[256,448]{1,0:T(8,128)} %get-tuple-element.5.refs_2_) | copy-start | bytes 1376260
  36.1 0.9 %copy-start.3 = (f32[256,256]{1,0:T(8,128)S(1)}, f32[256,256]{1,0:T(8,128)}, u32[]{:S(2)}) copy-start(f32[256,256]{1,0:T(8,128)} %get-tuple-element.6.refs_3_) | copy-start | bytes 786436

commit v6 on v5

--- a/solution.py
+++ b/solution.py
@@ -298,6 +298,7 @@
         copy.start()
         sent.append(copy)
 
+    rx, ry, rd = at.cross()
     whole = proj[...]
     gp[...] = dot(whole, whole, 0, 0).reshape(gp.shape)
     back = dot(bmean[...], whole, 0, 0)
@@ -326,9 +327,22 @@
         go(remote(gram.at[at.p], gram.at[at.p], h_send.at[d - 1], h_recv.at[at.p], where))
 
     def forward(f, i):
-        for d in range(1, R):
-            q, where = at.rep(d)
-            go(remote(full.at[at.r, f], full.at[at.r, f], r_send.at[i, d - 1], r_recv.at[at.r, f], where))
+        slot = full.at[at.r, f]
+        for e, k in enumerate((rx, ry)):
+            go(remote(slot, slot, r_send.at[i, e], r_recv.at[at.r, f], {"replica": k}))
+
+    def arrive(k, g):
+        slot = full.at[k, g]
+        remote(slot, slot, r_send.at[0, 0], r_recv.at[k, g], {"replica": rx}).wait_recv()
+
+    def cross_on(i):
+        g = at.line_from(i)
+        arrive(rx, g)
+        arrive(ry, g)
+        odd = lax.rem(g, 2)
+        src = rx + (ry - rx) * odd
+        slot = full.at[src, g]
+        go(remote(slot, slot, r_send.at[i, 2], r_recv.at[src, g], {"replica": ry + (rx - ry) * odd}))
 
     def reduced():
         for d in range(1, F):
@@ -360,22 +374,26 @@
     steps = rank // b
     later = steps // 2
     moved = 1
+    crossed = 0
     for i in range(steps):
         factor_step(w, i * b, b)
         if later <= i + 1 < steps:
             until = F if i + 2 == steps else moved + max(1, (F - 1) // (steps - later))
             for d in range(moved, min(until, F)):
                 gathered(d)
+            if crossed < moved:
+                cross_on(crossed)
+                crossed += 1
             moved = min(until, F)
+    for i in range(crossed, F):
+        cross_on(i)
     inverse = w[:, rank:]
     ortho = dot(whole, inverse, 1, 1)
     left_out[...] = ortho * math.sqrt(rows * F)
     squares = jnp.zeros((1, rank), F32)
     for i in range(F):
         g = at.line_from(i)
-        for d in range(1, R):
-            k = at.rep_from(d)
-            remote(full.at[k, g], full.at[k, g], r_send.at[i, d - 1], r_recv.at[k, g], at.rep(d)[1]).wait_recv()
+        arrive(rd, g)
         v = dot(jnp.concatenate([full[k, g] for k in range(R)], axis=0), inverse, 1, 1)
         squares = squares + jnp.sum(v * v, axis=0, keepdims=True)
         for k in range(R):

time: 91.4 us -> 89.8 us (0.982)
  Pallas kernels: 85.8 us -> 83.6 us
    pallas_call x1, Pallas kernels: 51.4 us -> 49.3 us  [shards(): pl.pallas_call(lambda *refs: back_kernel(R, F, T, *refs), out_shape=(sds(...]
where the time goes in v6:
time: 89.8 us; the launch traced here: 89 us
  Pallas kernels  83.6 us (93%)
  local copies, waits for them, and re-layouts  4.69 us (5%)
    pallas_call x1, Pallas kernels, shards(): pl.pallas_call(lambda *refs: back_kernel(R, F, T, *refs), out_shape=(sds(...  49.3 us
    pallas_call x1, Pallas kernels, shards(): pl.pallas_call(lambda *refs: project_kernel(R, F, T, *refs), out_shape=(s...  34.4 us
    unnamed x11, local copies, waits for them, and re-layouts  4.69 us

profile of v6, /device:TPU:17, one launch (start us, length us, event | category | flops | bytes accessed | tf_op | source)
XLA Modules:
  0.0 89.0 jit_solution(8867089983150097597)
XLA Ops:
  0.6 0.0 copy-start.1
  0.6 0.0 copy-start
  0.7 34.4 %project.1 = (f32[256,448]{1,0:T(8,128)}, f32[256,256]{1,0:T(8,128)}) custom-call(f32[1,256,1792]{2,1,0:T(8,128)} %refs_0_.3, bf16[1,256,1792]{2,1,0:T(8,128)(2,1)} %refs_1_.3, f32[448,256]{1,0:T(8,128)} %refs_2_.1), custom_call_target="tpu_custom_call" | custom-call | tf_op jit(solution)/shard_map/project/pallas_call | solution.py:448
  35.0 0.0 copy-done.1
  35.0 0.0 copy-done
  35.1 0.0 copy-start.2
  35.1 1.0 %copy-done.2 = f32[256,448]{1,0:T(8,128)S(1)} copy-done((f32[256,448]{1,0:T(8,128)S(1)}, f32[256,448]{1,0:T(8,128)}, u32[]{:S(2)}) %copy-start.2) | copy-done | bytes 458776
  36.1 0.0 copy-start.3
  36.1 0.9 %copy-done.3 = f32[256,256]{1,0:T(8,128)S(1)} copy-done((f32[256,256]{1,0:T(8,128)S(1)}, f32[256,256]{1,0:T(8,128)}, u32[]{:S(2)}) %copy-start.3) | copy-done | bytes 262168
  37.1 49.3 %back.1 = (f32[256,256]{1,0:T(8,128)S(1)}, f32[448,256]{1,0:T(8,128)S(1)}, f32[1,256,1792]{2,1,0:T(8,128)S(1)}) custom-call(f32[1,256,1792]{2,1,0:T(8,128)S(1)} %copy-done, bf16[1,256,1792]{2,1,0:T(8,128)(2,1)S(1)} %copy-done.1, f32[256,448]{1,0:T(8,128)S(1)} %copy-done.2, f32[256,256]{1,0:T(8,128)S(1)} %copy-done.3), custom_call_target="tpu_custom_call" | custom-call | tf_op jit(solution)/shard_map/back/pallas_call | solution.py:471
  86.3 0.7 copy.9
  87.0 0.8 copy.10
  87.8 1.2 %copy.11 = f32[1,256,1792]{2,1,0:T(8,128)} copy(f32[1,256,1792]{2,1,0:T(8,128)S(1)} %get-tuple-element.12) | data formatting | bytes 3670016
Async XLA Ops:
  0.6 34.4 %copy-start.1 = (bf16[1,256,1792]{2,1,0:T(8,128)(2,1)S(1)}, bf16[1,256,1792]{2,1,0:T(8,128)(2,1)}, u32[]{:S(2)}) copy-start(bf16[1,256,1792]{2,1,0:T(8,128)(2,1)} %refs_1_.3) | copy-start | bytes 2752516
  0.6 34.4 %copy-start = (f32[1,256,1792]{2,1,0:T(8,128)S(1)}, f32[1,256,1792]{2,1,0:T(8,128)}, u32[]{:S(2)}) copy-start(f32[1,256,1792]{2,1,0:T(8,128)} %refs_0_.3) | copy-start | bytes 5505028
  35.1 1.0 %copy-start.2 = (f32[256,448]{1,0:T(8,128)S(1)}, f32[256,448]{1,0:T(8,128)}, u32[]{:S(2)}) copy-start(f32[256,448]{1,0:T(8,128)} %get-tuple-element.5.refs_2_) | copy-start | bytes 1376260
  36.1 0.9 %copy-start.3 = (f32[256,256]{1,0:T(8,128)S(1)}, f32[256,256]{1,0:T(8,128)}, u32[]{:S(2)}) copy-start(f32[256,256]{1,0:T(8,128)} %get-tuple-element.6.refs_3_) | copy-start | bytes 786436

commit v7 on v6

--- a/solution.py
+++ b/solution.py
@@ -372,7 +372,7 @@
     w[:, rank:] = jnp.where(ids == lanes, 1.0, 0.0).astype(F32)
     b = 64
     steps = rank // b
-    later = steps // 2
+    later = 1
     moved = 1
     crossed = 0
     for i in range(steps):

time: 89.8 us -> 90.8 us (1.011)
  Pallas kernels: 83.6 us -> 85.2 us
    pallas_call x1, Pallas kernels: 49.3 us -> 50.8 us  [shards(): pl.pallas_call(lambda *refs: back_kernel(R, F, T, *refs), out_shape=(sds(...]
where the time goes in v7:
time: 90.8 us; the launch traced here: 90.6 us
  Pallas kernels  85.2 us (94%)
  local copies, waits for them, and re-layouts  4.69 us (5%)
    pallas_call x1, Pallas kernels, shards(): pl.pallas_call(lambda *refs: back_kernel(R, F, T, *refs), out_shape=(sds(...  50.8 us
    pallas_call x1, Pallas kernels, shards(): pl.pallas_call(lambda *refs: project_kernel(R, F, T, *refs), out_shape=(s...  34.4 us
    unnamed x11, local copies, waits for them, and re-layouts  4.69 us

profile of v7, /device:TPU:17, one launch (start us, length us, event | category | flops | bytes accessed | tf_op | source)
XLA Modules:
  0.0 90.6 jit_solution(726112017249206242)
XLA Ops:
  0.6 0.0 copy-start.1
  0.6 0.0 copy-start
  0.7 34.4 %project.1 = (f32[256,448]{1,0:T(8,128)}, f32[256,256]{1,0:T(8,128)}) custom-call(f32[1,256,1792]{2,1,0:T(8,128)} %refs_0_.3, bf16[1,256,1792]{2,1,0:T(8,128)(2,1)} %refs_1_.3, f32[448,256]{1,0:T(8,128)} %refs_2_.1), custom_call_target="tpu_custom_call" | custom-call | tf_op jit(solution)/shard_map/project/pallas_call | solution.py:448
  35.0 0.0 copy-done.1
  35.0 0.0 copy-done
  35.1 0.0 copy-start.2
  35.1 1.0 %copy-done.2 = f32[256,448]{1,0:T(8,128)S(1)} copy-done((f32[256,448]{1,0:T(8,128)S(1)}, f32[256,448]{1,0:T(8,128)}, u32[]{:S(2)}) %copy-start.2) | copy-done | bytes 458776
  36.1 0.0 copy-start.3
  36.1 0.9 %copy-done.3 = f32[256,256]{1,0:T(8,128)S(1)} copy-done((f32[256,256]{1,0:T(8,128)S(1)}, f32[256,256]{1,0:T(8,128)}, u32[]{:S(2)}) %copy-start.3) | copy-done | bytes 262168
  37.1 50.8 %back.1 = (f32[256,256]{1,0:T(8,128)S(1)}, f32[448,256]{1,0:T(8,128)S(1)}, f32[1,256,1792]{2,1,0:T(8,128)S(1)}) custom-call(f32[1,256,1792]{2,1,0:T(8,128)S(1)} %copy-done, bf16[1,256,1792]{2,1,0:T(8,128)(2,1)S(1)} %copy-done.1, f32[256,448]{1,0:T(8,128)S(1)} %copy-done.2, f32[256,256]{1,0:T(8,128)S(1)} %copy-done.3), custom_call_target="tpu_custom_call" | custom-call | tf_op jit(solution)/shard_map/back/pallas_call | solution.py:471
  87.9 0.7 copy.9
  88.6 0.8 copy.10
  89.4 1.2 %copy.11 = f32[1,256,1792]{2,1,0:T(8,128)} copy(f32[1,256,1792]{2,1,0:T(8,128)S(1)} %get-tuple-element.12) | data formatting | bytes 3670016
Async XLA Ops:
  0.6 34.4 %copy-start.1 = (bf16[1,256,1792]{2,1,0:T(8,128)(2,1)S(1)}, bf16[1,256,1792]{2,1,0:T(8,128)(2,1)}, u32[]{:S(2)}) copy-start(bf16[1,256,1792]{2,1,0:T(8,128)(2,1)} %refs_1_.3) | copy-start | bytes 2752516
  0.6 34.4 %copy-start = (f32[1,256,1792]{2,1,0:T(8,128)S(1)}, f32[1,256,1792]{2,1,0:T(8,128)}, u32[]{:S(2)}) copy-start(f32[1,256,1792]{2,1,0:T(8,128)} %refs_0_.3) | copy-start | bytes 5505028
  35.1 1.0 %copy-start.2 = (f32[256,448]{1,0:T(8,128)S(1)}, f32[256,448]{1,0:T(8,128)}, u32[]{:S(2)}) copy-start(f32[256,448]{1,0:T(8,128)} %get-tuple-element.5.refs_2_) | copy-start | bytes 1376260
  36.1 0.9 %copy-start.3 = (f32[256,256]{1,0:T(8,128)S(1)}, f32[256,256]{1,0:T(8,128)}, u32[]{:S(2)}) copy-start(f32[256,256]{1,0:T(8,128)} %get-tuple-element.6.refs_3_) | copy-start | bytes 786436
